TPU v7x, 256 devices: a whole 4x4x8 slice. The times are simulated.
256 devices in a mesh: cell: 64 (over z, y, core), cuts: 4 (over x).
Axes of the slice: x: 4, y: 4, z: 8, core: 2. Of those that a mesh axis runs over, the one named last changes fastest.
Arguments:
- node_positions: float32 [3, 262144], P(None, 'cell'), may hold values from -7 to 13
- connectivity: int32 [2, 262144], P(None, 'cell'), may hold values from 0 to 4095, as said below
- burgers_index: int32 [2048], P('cell'), may hold values from 0 to 5
- applied_stress: float32 [3, 3], replicated, may hold values from -4 to 4
- ghost_request: int32 [64, 64, 4], P('cell'), may hold values from -1 to 31, as said below
- pair_list: int32 [2, 65536], P(None, ('cell', 'cuts')), may hold values from -1 to 287, as said below
Outputs:
- velocity: float32 [3, 262144], P(None, 'cell')
Inputs may be any that keep to these rules, and one draw needn't show every extreme that they name: `connectivity`: column s holds the two end nodes of segment s, numbered among the 4096 nodes of the same index of cell; each block of 128 segments is one closed loop, and every node is an end of exactly two segments. `ghost_request`: entry [c, o, t] names a block of index o of cell, numbered among its 32 blocks, that index c of cell uses, or -1 for an unused slot; in each row the used slots come first, and at least one slot of each row is used. `pair_list`: each device's 256 columns are its pair rows. A used row holds a block number below 32 of the device's cell index, then either such a block number or 32 + o * 4 + t for a used slot t of owner o in ghost_request. Empty rows hold -1 twice and come after all used rows; on each index of cell one device along cuts uses all its rows.
All inputs are finite; a program needn't handle non-finite values.
Results may differ from a plain program's by a relative error of at most 0.00027.
Values sent between devices are 32-bit elements; how exact they have to be, the bound alone decides.
A program may use at most 64 MiB of HBM per device.

v0:
```python
import jax
import jax.numpy as jnp
from jax import lax
from jax.sharding import PartitionSpec as P

MU_FACTOR = 10.0
CORE_SQUARED = 0.25
DRAG_FACTOR = 1.0
group_rows = 16


def burgers_table():
    scale_half = 0.5**0.5
    return (
        jnp.array(
            [
                [1.0, 1.0, 1.0, 1.0, 0.0, 0.0],
                [1.0, -1.0, 0.0, 0.0, 1.0, 1.0],
                [0.0, 0.0, 1.0, -1.0, 1.0, -1.0],
            ],
            jnp.float32,
        )
        * scale_half
    )


def block_data(positions, end_links, burgers, seg_count):
    block_count = burgers.shape[0]
    start = jnp.take(positions, end_links[0], axis=1)
    finish = jnp.take(positions, end_links[1], axis=1)
    middle = 0.5 * (start + finish)
    line_vectors = finish - start
    choose = (burgers[None, :] == jnp.arange(6, dtype=jnp.int32)[:, None]).astype(jnp.float32)
    vectors = jnp.dot(burgers_table(), choose, precision=lax.Precision.HIGHEST)
    line_blocks = line_vectors.reshape(3, block_count, seg_count)
    coupling = vectors[:, None, :, None] * line_blocks[None, :, :, :]
    coupling = coupling.reshape(9, block_count, seg_count)
    packed = jnp.concatenate([middle.reshape(3, block_count, seg_count), coupling], axis=0)
    return (jnp.transpose(packed, (1, 0, 2)), vectors, line_vectors)


def pair_forces(near_data, far_data, pair_scale):
    separation = near_data[:, :3, :, None] - far_data[:, :3, None, :]
    dist_sq = jnp.sum(separation * separation, axis=1) + CORE_SQUARED
    coupling = jnp.einsum(
        "gci,gcj->gij", near_data[:, 3:], far_data[:, 3:], precision=lax.Precision.HIGHEST
    )
    weight = MU_FACTOR * pair_scale[:, None, None] * coupling / (dist_sq * jnp.sqrt(dist_sq))
    on_first = jnp.sum(weight[:, None] * separation, axis=3)
    on_second = -jnp.sum(weight[:, None] * separation, axis=2)
    return (on_first, on_second)


def nodal_velocity(seg_force, line_vectors, end_links):
    node_total = end_links.shape[1]
    zero_field = jnp.zeros((3, node_total), jnp.float32)
    node_force = 0.5 * (
        zero_field.at[:, end_links[0]].add(seg_force)
        + zero_field.at[:, end_links[1]].add(seg_force)
    )
    length = jnp.sqrt(jnp.sum(line_vectors * line_vectors, axis=0) + CORE_SQUARED)
    flat_zero = jnp.zeros((node_total,), jnp.float32)
    drag_sum = (
        DRAG_FACTOR
        * 0.5
        * (flat_zero.at[end_links[0]].add(length) + flat_zero.at[end_links[1]].add(length))
    )
    return node_force / drag_sum[None, :]


def serve_blocks(block_rows, asked_slots):
    block_count = block_rows.shape[0]
    picked = block_rows[jnp.clip(asked_slots, 0, block_count - 1)]
    return picked * (asked_slots >= 0).astype(jnp.float32)[:, :, None, None]


def body(node_positions, connectivity, burgers_index, applied_stress, ghost_request, pair_list):
    block_count = burgers_index.shape[0]
    seg_count = node_positions.shape[1] // block_count
    blocks, vectors, line_vectors = block_data(
        node_positions, connectivity, burgers_index, seg_count
    )
    cell_count = lax.axis_size("cell")
    slot_count = ghost_request.shape[2]
    my_cell = lax.axis_index("cell")
    wanted = ghost_request[0]
    asked_slots = lax.all_to_all(wanted, "cell", split_axis=0, concat_axis=0, tiled=True)
    ghost_blocks = lax.all_to_all(
        serve_blocks(blocks, asked_slots), "cell", split_axis=0, concat_axis=0, tiled=True
    )
    live_count = jnp.sum((pair_list[0] >= 0).astype(jnp.int32))
    everything = jnp.concatenate(
        [blocks, ghost_blocks.reshape(cell_count * slot_count, 12, seg_count)], axis=0
    )
    all_count = everything.shape[0]
    flat_wanted = wanted.reshape(cell_count * slot_count)
    group_count = (live_count + group_rows - 1) // group_rows

    def one_group(step_index, forces):
        window = lax.dynamic_slice_in_dim(pair_list, step_index * group_rows, group_rows, 1)
        first_idx = window[0]
        second_idx = window[1]
        alive = first_idx >= 0
        first_safe = jnp.clip(first_idx, 0, block_count - 1)
        second_safe = jnp.clip(second_idx, 0, all_count - 1)
        ghost_slot = jnp.clip(second_idx - block_count, 0, cell_count * slot_count - 1)
        same_block = (second_idx == first_idx) | (second_idx >= block_count) & (
            ghost_slot // slot_count == my_cell
        ) & (flat_wanted[ghost_slot] == first_idx)
        pair_scale = jnp.where(alive, jnp.where(same_block, 0.5, 1.0), 0.0).astype(jnp.float32)
        on_first, on_second = pair_forces(
            everything[first_safe], everything[second_safe], pair_scale
        )
        return forces.at[first_safe].add(on_first).at[second_safe].add(on_second)

    forces = lax.fori_loop(
        0, group_count, one_group, jnp.zeros((all_count, 3, seg_count), jnp.float32)
    )
    local_force = forces[:block_count]
    ghost_force = forces[block_count:].reshape(cell_count, slot_count, 3, seg_count)
    returned = lax.all_to_all(ghost_force, "cell", split_axis=0, concat_axis=0, tiled=True)
    targets = jnp.clip(asked_slots, 0, block_count - 1).reshape(-1)
    weights = (asked_slots >= 0).astype(jnp.float32).reshape(-1)
    returned = returned.reshape(-1, 3, seg_count) * weights[:, None, None]
    local_force = local_force.at[targets].add(returned)
    block_force = lax.psum(local_force, "cuts")
    seg_force = jnp.transpose(block_force, (1, 0, 2)).reshape(3, block_count * seg_count)
    symmetric = 0.5 * (applied_stress + applied_stress.T)
    traction = jnp.dot(symmetric, vectors, precision=lax.Precision.HIGHEST)
    traction = jnp.repeat(traction, seg_count, axis=1)
    seg_force = seg_force + jnp.cross(traction, line_vectors, axis=0)
    return nodal_velocity(seg_force, line_vectors, connectivity)


def solution(mesh):
    in_specs = (
        P(None, "cell"),
        P(None, "cell"),
        P("cell"),
        P(),
        P("cell", None, None),
        P(None, ("cell", "cuts")),
    )
    out_specs = P(None, "cell")
    return jax.shard_map(body, mesh=mesh, in_specs=in_specs, out_specs=out_specs, check_vma=False)
```

profile of v0, /device:TPU:1, one launch (start us, length us, event | category | flops | bytes accessed | tf_op | source)
XLA Modules:
  0.0 508.5 jit_solution(7839235417331046002)
XLA Ops:
  1.4 13.2 %all-to-all-start = ((s32[64,1,4]{2,1,0:T(1,128)}), s32[64,1,4]{2,1,0:T(1,128)S(1)}, u32[]{:S(2)}, u32[]{:S(2)}) async-start(s32[64,1,4]{2,1,0:T(1,128)} %bitcast.17), calls=%async_computation | async-start | bytes 65536 | tf_op jit(solution)/shard_map/all_to_all | solution.py:87
  16.9 14.1 %gather_fusion.4 = f32[4096,3]{1,0:T(8,128)} fusion(f32[3,4096]{0,1:T(8,128)S(1)} %copy.126, s32[4096]{0:T(1024)S(1)} %fusion.18), kind=kCustom, calls=%fused_computation.clone | custom fusion | bytes 114688 | tf_op jit(solution)/shard_map/jit(_take)/gather | solution.py:29
  31.0 2.2 copy.127
  33.2 14.1 %gather_fusion.5 = f32[4096,3]{1,0:T(8,128)} fusion(f32[3,4096]{0,1:T(8,128)S(1)} %copy.126, s32[4096]{0:T(1024)S(1)} %fusion.19), kind=kCustom, calls=%fused_computation.4.clone | custom fusion | bytes 114688 | tf_op jit(solution)/shard_map/jit(_take)/gather | solution.py:30
  47.3 2.2 copy.129
  53.9 10.4 %all-to-all-start.1 = ((f32[64,4,12,128]{3,1,2,0:T(4,128)}), f32[64,4,12,128]{3,1,2,0:T(4,128)S(1)}, u32[]{:S(2)}, u32[]{:S(2)}) async-start(f32[64,4,12,128]{3,1,2,0:T(4,128)} %copy_multiply_fusion), calls=%async_computation.1 | async-start | bytes 3145728 | tf_op jit(solution)/shard_map/all_to_all | solution.py:88
  69.0 34.2 %all-to-all-done.1 = f32[64,4,12,128]{3,1,2,0:T(4,128)S(1)} async-done(((f32[64,4,12,128]{3,1,2,0:T(4,128)}), f32[64,4,12,128]{3,1,2,0:T(4,128)S(1)}, u32[]{:S(2)}, u32[]{:S(2)}) %all-to-all-start.1) | async-done | bytes 1572896 | tf_op jit(solution)/shard_map/all_to_all | solution.py:88
  105.7 69.4 %while.12 = (s32[]{:T(128)}, f32[288,3,128]{2,1,0:T(4,128)}, s32[]{:T(128)}, s32[2,256]{1,0:T(2,128)}, s32[]{:T(128)}, /*index=5*/s32[256]{0:T(256)S(1)}, f32[28...) while((s32[]{:T(128)}, f32[288,3,128]{2,1,0:T(4,128)}, s32[]{:T(128)}, ...), condition=%wide.region_7.9_spmd, body=%wide.region_1.8_spmd.sunk | while | flops 34612884 | bytes 5634295 | solution.py:116
  113.3 3.2 fusion.49
  116.5 2.1 fusion.50
  118.6 2.2 scatter_fusion
  120.8 2.1 scatter_fusion.1
  130.5 3.2 fusion.49
  133.7 2.1 fusion.50
  135.8 2.1 scatter_fusion
  137.9 2.1 scatter_fusion.1
  147.6 3.2 fusion.49
  150.8 2.1 fusion.50
  152.8 2.2 scatter_fusion
  155.0 2.1 scatter_fusion.1
  164.7 3.2 fusion.49
  167.9 2.1 fusion.50
  170.0 2.5 scatter_fusion
  172.6 2.5 scatter_fusion.1
  177.1 211.4 %all-to-all-start.2 = ((f32[64,4,3,128]{3,1,2,0:T(4,128)}), f32[64,4,3,128]{3,1,2,0:T(4,128)S(1)}, u32[]{:S(2)}, u32[]{:S(2)}) async-start(f32[64,4,3,128]{3,1,2,0:T(4,128)} %copy.139), calls=%async_computation.2 | async-start | bytes 786432 | tf_op jit(solution)/shard_map/all_to_all | solution.py:121
  388.5 22.0 %scatter_custom_fusion.5 = f32[4096]{0:T(1024)S(1)} fusion(s32[4096]{0:T(1024)} %bitcast.111, f32[4096]{0:T(1024)S(1)} %add_sqrt_fusion, f32[]{:T(128)} %constant.148.clone.1), kind=kCustom, calls=%fused_computation.80 | custom fusion | flops 4096 | bytes 16896 | tf_op jit(solution)/shard_map/scatter-add | solution.py:66
  410.6 22.1 %scatter_custom_fusion.6 = f32[4096]{0:T(1024)S(1)} fusion(s32[4096]{0:T(1024)} %bitcast.113, f32[4096]{0:T(1024)S(1)} %add_sqrt_fusion, f32[]{:T(128)} %constant.148.clone.1), kind=kCustom, calls=%fused_computation.78 | custom fusion | flops 4096 | bytes 16896 | tf_op jit(solution)/shard_map/scatter-add | solution.py:66
  434.3 8.6 %scatter_fusion.2 = f32[32,3,128]{2,1,0:T(4,128)S(1)} fusion(f32[32,3,128]{2,1,0:T(4,128)S(1)} %slice.82, s32[256]{0:T(256)S(1)} %bitcast.115, f32[256,3,128]{2,1,0:T(4,128)S(1)} %copy.141), kind=kCustom, calls=%fused_computation.8 | custom fusion | flops 98304 | bytes 1180672 | tf_op jit(solution)/shard_map/scatter-add | solution.py:125
  442.9 12.8 %psum.7 = f32[3,4096]{1,0:T(4,128)S(1)} all-reduce(f32[3,4096]{1,0:T(4,128)S(1)} %bitcast.96), channel_id=1, replica_groups=mesh['cell'=64,'cuts'=4] {'cuts'}, use_global_device_ids=true, to_apply=%region_9.11 | all-reduce | flops 12288 | bytes 98304 | tf_op jit(solution)/shard_map/psum | solution.py:126
  457.8 23.2 %scatter_custom_fusion.4 = f32[3,4096]{0,1:T(8,128)S(1)} fusion(s32[4096]{0:T(1024)} %bitcast.114, f32[4096,3]{1,0:T(8,128)} %copy.143, f32[]{:T(128)} %constant.148.clone.1), kind=kCustom, calls=%fused_computation.44 | custom fusion | flops 12288 | bytes 49664 | tf_op jit(solution)/shard_map/scatter-add | solution.py:59
  481.0 24.0 %scatter_custom_fusion.3 = f32[3,4096]{0,1:T(8,128)} fusion(s32[4096]{0:T(1024)} %bitcast.112, f32[4096,3]{1,0:T(8,128)} %copy.143, f32[]{:T(128)} %constant.148.clone.1), kind=kCustom, calls=%fused_computation.46 | custom fusion | flops 12288 | bytes 49664 | tf_op jit(solution)/shard_map/scatter-add | solution.py:58
  505.7 2.2 copy.145
  (142 shorter events, 51.6 us)
Async XLA Ops:
  1.4 49.3 %all-to-all-start = ((s32[64,1,4]{2,1,0:T(1,128)}), s32[64,1,4]{2,1,0:T(1,128)S(1)}, u32[]{:S(2)}, u32[]{:S(2)}) async-start(s32[64,1,4]{2,1,0:T(1,128)} %bitcast.17), calls=%async_computation | async-start | bytes 65536 | tf_op jit(solution)/shard_map/all_to_all | solution.py:87
  33.2 17.0 %copy-start.9 = (f32[3,6]{1,0:T(4,128)S(1)}, f32[3,6]{1,0:T(4,128)}, u32[]{:S(2)}) copy-start(f32[3,6]{1,0:T(4,128)} %constant.165) | copy-start | bytes 220
  33.2 17.0 %copy-start.10 = (s32[32]{0:T(128)S(1)}, s32[32]{0:T(128)}, u32[]{:S(2)}) copy-start(s32[32]{0:T(128)} %param.13) | copy-start | bytes 388
  53.9 13.4 %copy-start.8 = (f32[3,3]{1,0:T(4,128)S(1)}, f32[3,3]{1,0:T(4,128)}, u32[]{:S(2)}) copy-start(f32[3,3]{1,0:T(4,128)} %param.14) | copy-start | bytes 112
  53.9 13.8 %copy-start.1 = (s32[2,4096]{1,0:T(2,128)S(1)}, s32[2,4096]{1,0:T(2,128)}, u32[]{:S(2)}) copy-start(s32[2,4096]{1,0:T(2,128)} %param.12) | copy-start | bytes 98308
  53.9 49.4 %all-to-all-start.1 = ((f32[64,4,12,128]{3,1,2,0:T(4,128)}), f32[64,4,12,128]{3,1,2,0:T(4,128)S(1)}, u32[]{:S(2)}, u32[]{:S(2)}) async-start(f32[64,4,12,128]{3,1,2,0:T(4,128)} %copy_multiply_fusion), calls=%async_computation.1 | async-start | bytes 3145728 | tf_op jit(solution)/shard_map/all_to_all | solution.py:88
  107.1 3.7 copy-start.2
  107.6 1.2 copy-start
  113.3 5.3 %copy-start.3 = (s32[16]{0:T(128)S(1)}, s32[16]{0:T(128)}, u32[]{:S(2)}) copy-start(s32[16]{0:T(128)} %copy-done.2) | copy-start | bytes 196 | tf_op jit(solution)/shard_map/while
  124.2 3.7 copy-start.2
  124.8 1.2 copy-start
  130.5 5.3 %copy-start.3 = (s32[16]{0:T(128)S(1)}, s32[16]{0:T(128)}, u32[]{:S(2)}) copy-start(s32[16]{0:T(128)} %copy-done.2) | copy-start | bytes 196 | tf_op jit(solution)/shard_map/while
  141.3 3.7 copy-start.2
  141.9 1.2 copy-start
  147.6 5.3 %copy-start.3 = (s32[16]{0:T(128)S(1)}, s32[16]{0:T(128)}, u32[]{:S(2)}) copy-start(s32[16]{0:T(128)} %copy-done.2) | copy-start | bytes 196 | tf_op jit(solution)/shard_map/while
  158.5 3.7 copy-start.2
  159.0 1.2 copy-start
  164.7 5.3 %copy-start.3 = (s32[16]{0:T(128)S(1)}, s32[16]{0:T(128)}, u32[]{:S(2)}) copy-start(s32[16]{0:T(128)} %copy-done.2) | copy-start | bytes 196 | tf_op jit(solution)/shard_map/while
  175.1 213.4 %copy-start.4 = (f32[4096]{0:T(1024)S(1)}, f32[4096]{0:T(1024)}, u32[]{:S(2)}) copy-start(f32[4096]{0:T(1024)} %get-tuple-element.145) | copy-start | bytes 49156
  177.1 256.8 %all-to-all-start.2 = ((f32[64,4,3,128]{3,1,2,0:T(4,128)}), f32[64,4,3,128]{3,1,2,0:T(4,128)S(1)}, u32[]{:S(2)}, u32[]{:S(2)}) async-start(f32[64,4,3,128]{3,1,2,0:T(4,128)} %copy.139), calls=%async_computation.2 | async-start | bytes 786432 | tf_op jit(solution)/shard_map/all_to_all | solution.py:121
  433.8 21.9 %copy-start.5 = (f32[1,4096]{1,0:T(1,128)S(1)}, f32[1,4096]{1,0:T(1,128)}, u32[]{:S(2)}) copy-start(f32[1,4096]{1,0:T(1,128)} %get-tuple-element.153) | copy-start | bytes 49156
  433.8 21.9 %copy-start.6 = (f32[1,4096]{1,0:T(1,128)S(1)}, f32[1,4096]{1,0:T(1,128)}, u32[]{:S(2)}) copy-start(f32[1,4096]{1,0:T(1,128)} %get-tuple-element.154) | copy-start | bytes 49156
  433.8 21.9 %copy-start.7 = (f32[1,4096]{1,0:T(1,128)S(1)}, f32[1,4096]{1,0:T(1,128)}, u32[]{:S(2)}) copy-start(f32[1,4096]{1,0:T(1,128)} %get-tuple-element.155) | copy-start | bytes 49156
where the time goes:
time: 515 us; the launch traced here: 509 us
  starting transfers between devices  235 us (46%)
  other arithmetic  144 us (28%)
  local copies, waits for them, and re-layouts  67.7 us (13%)
  waiting for transfers between devices  34.3 us (7%)
  matrix products  13 us (3%)
  blocking collectives  12.8 us (2%)
    all_to_all x1, starting transfers between devices, body(): lax.all_to_all(ghost_force, 'cell', split_axis=0, concat_axis=0, tiled=True)  211 us
    all_to_all x1, waiting for transfers between devices, body(): lax.all_to_all(serve_blocks(blocks, asked_slots), 'cell', split_axis=0, c...  34.2 us
    scatter-add x1, other arithmetic, nodal_velocity(): zero_field.at[:, end_links[0]].add(seg_force)  24 us
    scatter-add x1, other arithmetic, nodal_velocity(): zero_field.at[:, end_links[1]].add(seg_force)  23.2 us
    scatter-add x1, other arithmetic, nodal_velocity(): flat_zero.at[end_links[1]].add(length)  22.1 us
    scatter-add x1, other arithmetic, nodal_velocity(): flat_zero.at[end_links[0]].add(length)  22 us
    scatter-add x8, other arithmetic, one_group(): return forces.at[first_safe].add(on_first).at[second_safe].add(on_second)  17.8 us
    gather x2, local copies, waits for them, and re-layouts, block_data(): finish = jnp.take(positions, end_links[1], axis=1)  16.3 us
  transfers between devices with their start and end apart: 3, of which 1 were waited for; matrix products, arithmetic and copies ran while one was open for 17% of the time, Pallas kernels for 0%

commit v1 on v0

v1 whole, which is shorter than its diff:
```python
import functools

import jax
import jax.numpy as jnp
from jax import lax
from jax.experimental import pallas as pl
from jax.experimental.pallas import tpu as pltpu
from jax.sharding import PartitionSpec as P

SEG = 128
COMPS = 9
ROWS = 16
UNROLL = 4
MU_FACTOR = 10.0
CORE_SQUARED = 0.25
HALF_ROOT = 0.5**0.5
MESH = pl.DeviceIdType.MESH
F32 = jnp.float32
BF16 = jnp.bfloat16
I32 = jnp.int32
VMEM = pl.BlockSpec(memory_space=pltpu.VMEM)
SMEM = pl.BlockSpec(memory_space=pltpu.SMEM)
NN = (((1,), (0,)), ((), ()))
NT = (((1,), (1,)), ((), ()))


def iota(shape, axis):
    return lax.broadcasted_iota(I32, shape, axis)


def dot(a, b, dims):
    return lax.dot_general(a, b, dims, preferred_element_type=F32)


def split(value, parts):
    pieces = []
    rest = value
    for part in range(parts):
        piece = rest.astype(BF16)
        pieces.append(piece)
        if part < parts - 1:
            rest = rest - piece.astype(F32)
    return pieces


def prep_kernel(pos, conn, burg, req, data, table, reqb, links):
    blocks = data.shape[0]
    for end in range(2):
        for b in range(blocks):
            links[end, b : b + 1, :] = conn[end : end + 1, b * SEG : (b + 1) * SEG]
    low = [links[end] & (SEG - 1) for end in range(2)]
    high = [links[end] >> 7 for end in range(2)]

    def step(h, carry):
        lanes = pl.ds(pl.multiple_of(h * SEG, SEG), SEG)
        out = []
        for end in range(2):
            hit = high[end] == h
            for c in range(3):
                row = jnp.broadcast_to(pos[c : c + 1, lanes], (blocks, SEG))
                got = jnp.take_along_axis(row, low[end], axis=1)
                out.append(jnp.where(hit, got, carry[end * 3 + c]))
        return tuple(out)

    zero = jnp.zeros((blocks, SEG), F32)
    ends = lax.fori_loop(0, pos.shape[1] // SEG, step, (zero,) * 6)
    comps = [0.5 * (ends[c] + ends[3 + c]) for c in range(3)]
    comps += [ends[3 + c] - ends[c] for c in range(3)]
    diagonal = iota((blocks, blocks), 0) == iota((blocks, blocks), 1)
    spread = jnp.where(diagonal, jnp.broadcast_to(burg[...], (blocks, blocks)), 0)
    kind = jnp.broadcast_to(jnp.sum(spread, axis=1, keepdims=True), (blocks, SEG))
    odd = jnp.where((kind & 1) == 1, -HALF_ROOT, HALF_ROOT)
    comps.append(jnp.where(kind < 4, HALF_ROOT, 0.0))
    comps.append(jnp.where(kind < 2, odd, jnp.where(kind < 4, 0.0, HALF_ROOT)))
    comps.append(jnp.where(kind < 2, 0.0, odd))
    table[...] = jnp.zeros(table.shape, table.dtype)
    for c in range(COMPS):
        lanes = slice(c * SEG, (c + 1) * SEG)
        data[:, lanes] = comps[c]
        for part, piece in enumerate(split(comps[c], 3)):
            table[part * blocks : (part + 1) * blocks, lanes] = piece
    reqb[...] = jnp.full(reqb.shape, -1, I32)
    owners, cap = req.shape
    for t in range(cap):
        reqb[pl.ds(t, owners, stride=8), :] = jnp.broadcast_to(req[:, t : t + 1], (owners, SEG))


def greet(me, cut, rho, groups, cuts):
    barrier = pltpu.get_barrier_semaphore()

    def step(m, carry):
        other = m * cuts + rho

        @pl.when(other != me)
        def _():
            pl.semaphore_signal(barrier, inc=1, device_id=(other, cut), device_id_type=MESH)

        return carry

    lax.fori_loop(0, groups, step, 0)
    for d in range(1, cuts):
        peer = lax.rem(cut + d, cuts)
        pl.semaphore_signal(barrier, inc=1, device_id=(me, peer), device_id_type=MESH)
    own = jnp.where(rho == lax.rem(me, cuts), 1, 0)
    pl.semaphore_wait(barrier, groups + cuts - 1 - own)


def for_partners(me, rho, groups, cuts, run):
    def step(m, carry):
        other = m * cuts + rho

        @pl.when(other != me)
        def _():
            run(m, other)

        return carry

    lax.fori_loop(0, groups, step, 0)


def prefix(flags):
    rows, lanes = flags.shape
    value = jnp.where(flags, 1.0, 0.0).astype(F32)
    coded = value.astype(BF16)
    upper = jnp.where(iota((lanes, lanes), 0) <= iota((lanes, lanes), 1), 1.0, 0.0).astype(BF16)
    along = dot(coded, upper, NN)
    ones = jnp.ones((lanes, lanes), BF16)
    totals = dot(coded, ones, NN)
    row = iota((rows, lanes), 0)
    offset = jnp.zeros((rows, lanes), F32)
    for r in range(rows - 1):
        offset = offset + jnp.where(row > r, jnp.broadcast_to(totals[r : r + 1, :], (rows, lanes)), 0.0)
    return (along - value + offset).astype(I32)


def count(flags):
    value = jnp.where(flags, 1.0, 0.0).astype(F32)
    return jnp.sum(jnp.sum(value, axis=1, keepdims=True), axis=0, keepdims=True).astype(I32)


def share_pairs(first, second, own_rows, me, cut, cuts, cap, blocks):
    alive = first >= 0
    ghost = second >= blocks
    slot = jnp.maximum(second - blocks, 0)
    owner = slot >> 2
    part = slot & 3
    own = ghost & (owner == me)
    far = ghost & (owner != me)
    wanted = jnp.zeros_like(second)
    for t in range(cap):
        row = jnp.broadcast_to(own_rows[t : t + 1, :], second.shape)
        wanted = jnp.where(part == t, row, wanted)
    near_block = jnp.where(own, wanted, second)
    block = jnp.where(far, blocks + (owner >> 2) * cap + part, near_block)
    half = jnp.logical_and(jnp.logical_not(far), block == first)
    place = (owner + me) & 3
    far_alive = alive & far
    near_alive = alive & jnp.logical_not(far)
    target = (count(alive) + cuts - 1) >> 2
    begin = jnp.zeros((1, 1), I32)
    low = begin
    top = begin
    for j in range(cuts):
        room = jnp.maximum(target - count(far_alive & (place == j)), 0)
        low = jnp.where(cut == j, begin, low)
        top = jnp.where(cut == j, begin + room, top)
        begin = begin + room
    rank = prefix(near_alive)
    mine = (far_alive & (place == cut)) | (near_alive & (rank >= low) & (rank < top))
    spot = prefix(mine)
    first_code = jnp.where(mine, first + jnp.where(half, 64, 32), 0).astype(F32)
    second_code = jnp.where(mine, block, 0).astype(F32)
    rows, lanes = first.shape
    codes = jnp.zeros((2 * rows, lanes), F32)
    for r in range(rows):
        at = spot[r : r + 1, :]
        hit = iota((rows, lanes), 0) == jnp.broadcast_to(at >> 7, (rows, lanes))
        left = jnp.concatenate(
            [
                jnp.where(hit, jnp.broadcast_to(first_code[r : r + 1, :], (rows, lanes)), 0.0),
                jnp.where(hit, jnp.broadcast_to(second_code[r : r + 1, :], (rows, lanes)), 0.0),
            ],
            axis=0,
        ).astype(BF16)
        chosen = iota((lanes, lanes), 0) == jnp.broadcast_to(at & (lanes - 1), (lanes, lanes))
        codes = codes + dot(left, jnp.where(chosen, 1.0, 0.0).astype(BF16), NT)
    return codes.astype(I32), count(mine)


def exchange_kernel(
    cuts, groups, cap, blocks,
    reqb, table, pairs,
    ghost, asked, codes,
    plist, stage, ordered, rsend, rrecv, psend, precv, bsend, brecv,
):
    me = lax.axis_index("cell")
    cut = lax.axis_index("cuts")
    rho = lax.rem(cut - lax.rem(me, cuts) + cuts, cuts)
    slot = lax.div(me, cuts)
    asked[...] = jnp.full(asked.shape, -1, I32)
    ghost[...] = jnp.zeros(ghost.shape, F32)
    plist[cut] = jnp.zeros(plist.shape[1:], I32)
    for e in range(2):
        for r in range(2):
            plist[cut, 2 * e + r : 2 * e + r + 1, :] = pairs[e : e + 1, r * SEG : (r + 1) * SEG]
    greet(me, cut, rho, groups, cuts)

    def request_copy(m, other):
        return pltpu.make_async_remote_copy(
            src_ref=reqb.at[pl.ds(pl.multiple_of(other * 8, 8), 8)],
            dst_ref=asked.at[pl.ds(pl.multiple_of(slot * 8, 8), 8)],
            send_sem=rsend.at[m],
            recv_sem=rrecv.at[slot],
            device_id=(other, cut),
            device_id_type=MESH,
        )

    def request_arrival(m, other):
        return pltpu.make_async_remote_copy(
            src_ref=reqb.at[pl.ds(pl.multiple_of(other * 8, 8), 8)],
            dst_ref=asked.at[pl.ds(pl.multiple_of(m * 8, 8), 8)],
            send_sem=rsend.at[m],
            recv_sem=rrecv.at[m],
            device_id=(other, cut),
            device_id_type=MESH,
        )

    def pair_copy(d, at):
        return pltpu.make_async_remote_copy(
            src_ref=plist.at[cut],
            dst_ref=plist.at[at],
            send_sem=psend.at[d - 1],
            recv_sem=precv.at[at],
            device_id=(me, lax.rem(cut + d, cuts)),
            device_id_type=MESH,
        )

    for_partners(me, rho, groups, cuts, lambda m, other: request_copy(m, other).start())
    for d in range(1, cuts):
        pair_copy(d, cut).start()
    for_partners(me, rho, groups, cuts, lambda m, other: request_arrival(m, other).wait_recv())

    wide = asked.shape[0]
    lane = iota((wide, SEG), 1)
    hit = ((lane & (blocks - 1)) == asked[...]) & (lane < 3 * blocks)
    onehot = jnp.where(hit, 1.0, 0.0).astype(BF16)
    for c in range(COMPS):
        lanes = slice(c * SEG, (c + 1) * SEG)
        got = dot(onehot, table[:, lanes], NN)
        for m in range(groups):
            stage[m, :, lanes] = got[m * 8 : m * 8 + cap, :]

    def block_copy(m, other, at):
        return pltpu.make_async_remote_copy(
            src_ref=stage.at[m],
            dst_ref=ghost.at[at],
            send_sem=bsend.at[m],
            recv_sem=brecv.at[at],
            device_id=(other, cut),
            device_id_type=MESH,
        )

    for_partners(me, rho, groups, cuts, lambda m, other: block_copy(m, other, slot).start())
    for d in range(1, cuts):
        pair_copy(d, lax.rem(cut - d + cuts, cuts)).wait_recv()
    for j in range(cuts):
        ordered[0, 2 * j : 2 * j + 2, :] = plist[j, 0:2, :]
        ordered[1, 2 * j : 2 * j + 2, :] = plist[j, 2:4, :]
    own_rows = reqb[pl.ds(pl.multiple_of(me * 8, 8), 8), :]
    listed, total = share_pairs(ordered[0], ordered[1], own_rows, me, cut, cuts, cap, blocks)
    codes[0:16, :] = listed
    codes[16:24, :] = jnp.broadcast_to(total, (8, SEG))
    for_partners(me, rho, groups, cuts, lambda m, other: block_copy(m, other, m).wait_recv())
    for_partners(me, rho, groups, cuts, lambda m, other: block_copy(m, other, m).wait_send())
    for_partners(me, rho, groups, cuts, lambda m, other: request_copy(m, other).wait_send())
    for d in range(1, cuts):
        pair_copy(d, cut).wait_send()


def pair_kernel(codes, data, ghost, near_force, far_force, everything, total, moments, columns):
    blocks = data.shape[0]
    groups, cap, _ = ghost.shape
    count_all = blocks + groups * cap

    def fill(target, row, value, start, rows):
        target[pl.ds(start * ROWS + row, rows, stride=ROWS), :] = value

    def fill_moments(values, start, rows):
        for c in range(3):
            for part, piece in enumerate(split(values[c], 3)):
                fill(moments, part * 3 + c, piece.astype(F32), start, rows)

    moments[...] = jnp.where((iota(moments.shape, 0) & (ROWS - 1)) == 9, 1.0, 0.0)
    total[...] = jnp.zeros(total.shape, F32)
    everything[...] = jnp.zeros(everything.shape, F32)
    values = [data[:, c * SEG : (c + 1) * SEG] for c in range(COMPS)]
    for c in range(COMPS):
        fill(everything, c, values[c], 0, blocks)
    fill_moments(values, 0, blocks)
    for m in range(groups):
        values = [ghost[m, :, c * SEG : (c + 1) * SEG] for c in range(COMPS)]
        for c in range(COMPS):
            fill(everything, c, values[c], blocks + m * cap, cap)
        fill_moments(values, blocks + m * cap, cap)

    def tile(ref, block, rows):
        return ref[pl.ds(pl.multiple_of(block * ROWS, ROWS), rows), :]

    def spread(block, carry):
        turned = jnp.transpose(tile(everything, block, 8))
        for c in range(6):
            columns[block, c] = jnp.broadcast_to(turned[:, c : c + 1], (SEG, SEG))
        return carry

    lax.fori_loop(0, blocks, spread, 0)

    def one_pair(index):
        code = codes[index >> 7, index & (SEG - 1)]
        second = codes[8 + (index >> 7), index & (SEG - 1)]
        first = code & 31
        kind = code >> 5
        scale = jnp.where(kind == 1, MU_FACTOR, jnp.where(kind == 2, 0.5 * MU_FACTOR, 0.0))
        near = tile(everything, first, ROWS)
        far = tile(everything, second, ROWS)
        match = near[6:7] * far[6:7] + near[7:8] * far[7:8] + near[8:9] * far[8:9]
        factor = match * scale
        middle = [far[c : c + 1] for c in range(3)]
        line = [far[3 + c : 4 + c] * factor for c in range(3)]
        high, low = [], []
        step = 32
        for start in range(0, SEG, step):
            rows = slice(start, start + step)
            r = [columns[first, c, rows, :] - middle[c] for c in range(3)]
            dist = r[0] * r[0] + CORE_SQUARED + r[1] * r[1] + r[2] * r[2]
            g = (
                columns[first, 3, rows, :] * line[0]
                + columns[first, 4, rows, :] * line[1]
                + columns[first, 5, rows, :] * line[2]
            )
            inverse = lax.rsqrt(dist)
            weight = g * inverse * (inverse * inverse)
            big, small = split(weight, 2)
            high.append(big)
            low.append(small)
        high = jnp.concatenate(high, axis=0)
        low = jnp.concatenate(low, axis=0)
        near_moments = tile(moments, first, ROWS).astype(BF16)
        far_moments = tile(moments, second, ROWS).astype(BF16)
        on_first = dot(
            jnp.concatenate([far_moments, far_moments], axis=1),
            jnp.concatenate([high, low], axis=1),
            NT,
        )
        on_second = dot(
            jnp.concatenate([near_moments, near_moments], axis=1),
            jnp.concatenate([high, low], axis=0),
            NN,
        )
        return first, second, on_first, on_second

    def body(step, carry):
        results = [one_pair(step * UNROLL + u) for u in range(UNROLL)]
        for first, second, on_first, on_second in results:
            at = pl.ds(pl.multiple_of(first * ROWS, ROWS), ROWS)
            total[at, :] = total[at, :] + on_first
            at = pl.ds(pl.multiple_of(second * ROWS, ROWS), ROWS)
            total[at, :] = total[at, :] + on_second
        return carry

    lax.fori_loop(0, (codes[16, 0] + UNROLL - 1) // UNROLL, body, 0)

    def take(ref, row, start, rows):
        return ref[pl.ds(start * ROWS + row, rows, stride=ROWS), :]

    def force(start, rows, c):
        weight = take(total, 9, start, rows)
        others = take(total, c, start, rows) + take(total, 3 + c, start, rows) + take(total, 6 + c, start, rows)
        return take(everything, c, start, rows) * weight - others

    for c in range(3):
        lanes = slice(c * SEG, (c + 1) * SEG)
        near_force[:, lanes] = force(0, blocks, c)
        for m in range(groups):
            far_force[m, :, lanes] = force(blocks + m * cap, cap, c)


def return_kernel(
    cuts, groups, cap, blocks,
    near_force, far_force, asked,
    result,
    back, table, shares, bsend, brecv, ssend, srecv,
):
    me = lax.axis_index("cell")
    cut = lax.axis_index("cuts")
    rho = lax.rem(cut - lax.rem(me, cuts) + cuts, cuts)
    slot = lax.div(me, cuts)
    back[...] = jnp.zeros(back.shape, F32)
    table[...] = jnp.zeros(table.shape, F32)
    greet(me, cut, rho, groups, cuts)

    def reaction_copy(m, other, at):
        return pltpu.make_async_remote_copy(
            src_ref=far_force.at[m],
            dst_ref=back.at[at],
            send_sem=bsend.at[m],
            recv_sem=brecv.at[at],
            device_id=(other, cut),
            device_id_type=MESH,
        )

    for_partners(me, rho, groups, cuts, lambda m, other: reaction_copy(m, other, slot).start())
    wide = asked.shape[0]
    hit = iota((wide, SEG), 1) == asked[...]
    onehot = jnp.transpose(jnp.where(hit, 1.0, 0.0))[:blocks, :].astype(BF16)
    for_partners(me, rho, groups, cuts, lambda m, other: reaction_copy(m, other, m).wait_recv())
    for m in range(groups):
        table[m * 8 : m * 8 + cap, :] = back[m]
    mine = near_force[...]
    for piece in split(table[...], 3):
        mine = mine + dot(onehot, piece, NN)
    shares[cut] = mine

    def share_copy(d, at):
        return pltpu.make_async_remote_copy(
            src_ref=shares.at[cut],
            dst_ref=shares.at[at],
            send_sem=ssend.at[d - 1],
            recv_sem=srecv.at[at],
            device_id=(me, lax.rem(cut + d, cuts)),
            device_id_type=MESH,
        )

    for d in range(1, cuts):
        share_copy(d, cut).start()
    for d in range(1, cuts):
        share_copy(d, lax.rem(cut - d + cuts, cuts)).wait_recv()
    added = shares[0]
    for j in range(1, cuts):
        added = added + shares[j]
    result[...] = added
    for d in range(1, cuts):
        share_copy(d, cut).wait_send()
    for_partners(me, rho, groups, cuts, lambda m, other: reaction_copy(m, other, m).wait_send())


def node_kernel(pair_force, data, conn, stress, velocity):
    blocks = data.shape[0]
    value = [data[:, c * SEG : (c + 1) * SEG] for c in range(COMPS)]
    line = value[3:6]
    burgers = value[6:9]
    sigma = [[0.5 * (stress[a, b] + stress[b, a]) for b in range(3)] for a in range(3)]
    pull = [sigma[a][0] * burgers[0] + sigma[a][1] * burgers[1] + sigma[a][2] * burgers[2] for a in range(3)]
    fields = []
    for c in range(3):
        u, v = (c + 1) % 3, (c + 2) % 3
        turned = pull[u] * line[v] - pull[v] * line[u]
        fields.append(pair_force[:, c * SEG : (c + 1) * SEG] + turned)
    fields.append(jnp.sqrt(line[0] * line[0] + line[1] * line[1] + line[2] * line[2] + CORE_SQUARED))
    pieces = [piece for field in fields for piece in split(field, 2)]
    sums = jnp.zeros((len(pieces) * blocks, SEG), F32)
    for b in range(blocks):
        left, right = [], []
        for end in range(2):
            node = conn[end : end + 1, b * SEG : (b + 1) * SEG]
            hit = iota((blocks, SEG), 0) == jnp.broadcast_to(node >> 7, (blocks, SEG))
            column = [
                jnp.where(hit, jnp.broadcast_to(piece[b : b + 1, :].astype(F32), (blocks, SEG)), 0.0)
                for piece in pieces
            ]
            left.append(jnp.concatenate(column, axis=0).astype(BF16))
            chosen = iota((SEG, SEG), 0) == jnp.broadcast_to(node & (SEG - 1), (SEG, SEG))
            right.append(jnp.where(chosen, 1.0, 0.0).astype(BF16))
        sums = sums + dot(jnp.concatenate(left, axis=1), jnp.concatenate(right, axis=1), NT)
    merged = [sums[2 * f * blocks : (2 * f + 1) * blocks] + sums[(2 * f + 1) * blocks : (2 * f + 2) * blocks] for f in range(4)]
    for c in range(3):
        speed = merged[c] / merged[3]
        for b in range(blocks):
            velocity[c : c + 1, b * SEG : (b + 1) * SEG] = speed[b : b + 1, :]


def body(cuts, node_positions, connectivity, burgers_index, applied_stress, ghost_request, pair_list):
    blocks = burgers_index.shape[0]
    owners, cap = ghost_request.shape[1:]
    groups = owners // cuts
    nodes = node_positions.shape[1]
    width = COMPS * SEG
    shape = jax.ShapeDtypeStruct
    data, table, reqb = pl.pallas_call(
        prep_kernel,
        name="segments",
        out_shape=(
            shape((blocks, width), F32),
            shape((SEG, width), BF16),
            shape((owners * 8, SEG), I32),
        ),
        in_specs=[VMEM] * 4,
        out_specs=(VMEM,) * 3,
        scratch_shapes=[pltpu.VMEM((2, blocks, SEG), I32)],
    )(node_positions, connectivity, burgers_index.reshape(1, blocks), ghost_request[0])
    dma = pltpu.SemaphoreType.DMA
    ghost, asked, codes = pl.pallas_call(
        functools.partial(exchange_kernel, cuts, groups, cap, blocks),
        name="exchange",
        out_shape=(
            shape((groups, cap, width), F32),
            shape((groups * 8, SEG), I32),
            shape((24, SEG), I32),
        ),
        in_specs=[VMEM] * 3,
        out_specs=(VMEM,) * 3,
        scratch_shapes=[
            pltpu.VMEM((cuts, 8, SEG), I32),
            pltpu.VMEM((groups, cap, width), F32),
            pltpu.VMEM((2, 8, SEG), I32),
            dma((groups,)), dma((groups,)), dma((cuts,)), dma((cuts,)), dma((groups,)), dma((groups,)),
        ],
        compiler_params=pltpu.CompilerParams(collective_id=0, has_side_effects=True),
    )(reqb, table, pair_list)
    total_blocks = blocks + groups * cap
    near_force, far_force = pl.pallas_call(
        pair_kernel,
        name="pairs",
        out_shape=(
            shape((blocks, 3 * SEG), F32),
            shape((groups, cap, 3 * SEG), F32),
        ),
        in_specs=[SMEM, VMEM, VMEM],
        out_specs=(VMEM,) * 2,
        scratch_shapes=[
            pltpu.VMEM((total_blocks * ROWS, SEG), F32),
            pltpu.VMEM((total_blocks * ROWS, SEG), F32),
            pltpu.VMEM((total_blocks * ROWS, SEG), F32),
            pltpu.VMEM((blocks, 6, SEG, SEG), F32),
        ],
        compiler_params=pltpu.CompilerParams(vmem_limit_bytes=32 * 1024 * 1024),
    )(codes, data, ghost)
    pair_force = pl.pallas_call(
        functools.partial(return_kernel, cuts, groups, cap, blocks),
        name="reactions",
        out_shape=shape((blocks, 3 * SEG), F32),
        in_specs=[VMEM] * 3,
        out_specs=VMEM,
        scratch_shapes=[
            pltpu.VMEM((groups, cap, 3 * SEG), F32),
            pltpu.VMEM((groups * 8, 3 * SEG), F32),
            pltpu.VMEM((cuts, blocks, 3 * SEG), F32),
            dma((groups,)), dma((groups,)), dma((cuts,)), dma((cuts,)),
        ],
        compiler_params=pltpu.CompilerParams(collective_id=1, has_side_effects=True),
    )(near_force, far_force, asked)
    return pl.pallas_call(
        node_kernel,
        name="nodes",
        out_shape=shape((3, nodes), F32),
        in_specs=[VMEM, VMEM, VMEM, SMEM],
        out_specs=VMEM,
    )(pair_force, data, connectivity, applied_stress)


def solution(mesh):
    in_specs = (
        P(None, "cell"),
        P(None, "cell"),
        P("cell"),
        P(),
        P("cell", None, None),
        P(None, ("cell", "cuts")),
    )
    return jax.shard_map(
        functools.partial(body, mesh.shape["cuts"]),
        mesh=mesh,
        in_specs=in_specs,
        out_specs=P(None, "cell"),
        check_vma=False,
    )
```

time: 515 us -> 81.2 us (0.16); the launches traced: 509 us -> 80.9 us
  starting transfers between devices: 235 us -> 0 us
  other arithmetic: 144 us -> 0 us
  Pallas kernels: 0 us -> 76.5 us
  local copies, waits for them, and re-layouts: 67.7 us -> 4.29 us
  waiting for transfers between devices: 34.3 us -> 0 us
  matrix products: 13 us -> 0 us
  blocking collectives: 12.8 us -> 0 us
    all_to_all x3 -> x0, starting transfers between devices: 235 us -> none  [the longest x1 211 us: body(): lax.all_to_all(ghost_force, 'cell', split_axis=0, concat_axis=0, tiled=True)]
    scatter-add x13 -> x0, other arithmetic: 118 us -> none  [the longest x1 24 us: nodal_velocity(): zero_field.at[:, end_links[0]].add(seg_force)]
    pallas_call x0 -> x5, Pallas kernels: none -> 76.5 us  [the longest x1 24 us: body(): pl.pallas_call(functools.partial(exchange_kernel, cuts, groups, cap, bloc...]
    gather x17 -> x0, local copies, waits for them, and re-layouts: 45.6 us -> none  [the longest x2 16.3 us: block_data(): finish = jnp.take(positions, end_links[1], axis=1)]
    all_to_all x3 -> x0, waiting for transfers between devices: 34.3 us -> none  [the longest x1 34.2 us: body(): lax.all_to_all(serve_blocks(blocks, asked_slots), 'cell', split_axis=0, c...]
    reduce_sum x10 -> x0, other arithmetic: 14.4 us -> none  [the longest x4 8.23 us: pair_forces(): on_second = -jnp.sum(weight[:, None] * separation, axis=2)]
    dot_general x6 -> x0, matrix products: 13 us -> none  [the longest x4 12.8 us: pair_forces(): jnp.einsum('gci,gcj->gij', near_data[:, 3:], far_data[:, 3:], precision=l...]
    psum x1 -> x0, blocking collectives: 12.8 us -> none  [body(): block_force = lax.psum(local_force, 'cuts')]
  transfers between devices with their start and end apart: 3 -> 0, of which waited for: 1 -> 0; matrix products, arithmetic and copies ran while one was open for 17% -> 0% of each run, Pallas kernels for 0% -> 0%
where the time goes in v1:
time: 81.2 us; the launch traced here: 80.9 us
  Pallas kernels  76.5 us (94%)
  local copies, waits for them, and re-layouts  4.29 us (5%)
    pallas_call x1, Pallas kernels, body(): pl.pallas_call(functools.partial(exchange_kernel, cuts, groups, cap, bloc...  24 us
    pallas_call x1, Pallas kernels, body(): pl.pallas_call(functools.partial(return_kernel, cuts, groups, cap, blocks...  23.7 us
    pallas_call x1, Pallas kernels, body(): pl.pallas_call(pair_kernel, name='pairs', out_shape=(shape((blocks, 3 * S...  20 us
    pallas_call x1, Pallas kernels, body(): pl.pallas_call(prep_kernel, name='segments', out_shape=(shape((blocks, wi...  6.04 us
    unnamed x11, local copies, waits for them, and re-layouts  4.29 us
    pallas_call x1, Pallas kernels, body(): pl.pallas_call(node_kernel, name='nodes', out_shape=shape((3, nodes), F32...  2.89 us

profile of v1, /device:TPU:1, one launch (start us, length us, event | category | flops | bytes accessed | tf_op | source)
XLA Modules:
  0.0 80.9 jit_solution(13994747591509960571)
XLA Ops:
  0.0 1.4 %copy.7 = s32[1,64,4]{2,1,0:T(8,128)} copy(s32[1,64,4]{1,2,0:T(4,128)} %param.10) | data formatting | bytes 2048 | tf_op args[4]
  1.4 6.0 %segments.1 = (f32[32,1152]{1,0:T(8,128)}, bf16[128,1152]{1,0:T(8,128)(2,1)}, s32[512,128]{1,0:T(8,128)}) custom-call(f32[3,4096]{1,0:T(4,128)} %pos.1, s32[2,4096]{1,0:T(2,128)} %conn.3, s32[1,32]{1,0:T(1,128)} %bitcast.3, s32[64,4]{1,0:T(8,128)} %bitcast.2), custom_call_target="tpu_custom_call" | custom-call | tf_op jit(solution)/shard_map/segments/pallas_call | solution.py:488
  7.4 0.0 copy-start
  7.4 24.0 %exchange.1 = (f32[16,4,1152]{2,1,0:T(4,128)}, s32[128,128]{1,0:T(8,128)}, s32[24,128]{1,0:T(8,128)}) custom-call(s32[512,128]{1,0:T(8,128)} %get-tuple-element.13.reqb, bf16[128,1152]{1,0:T(8,128)(2,1)} %get-tuple-element.14.table, s32[2,256]{1,0:T(2,128)} %pairs.2), custom_call_target="tpu_custom_call" | custom-call | tf_op jit(solution)/shard_map/exchange/pallas_call | solution.py:501
  31.4 0.0 copy-done
  31.4 0.0 copy-start.1
  31.4 1.0 %copy-done.1 = f32[16,4,1152]{2,1,0:T(4,128)S(1)} copy-done((f32[16,4,1152]{2,1,0:T(4,128)S(1)}, f32[16,4,1152]{2,1,0:T(4,128)}, u32[]{:S(2)}) %copy-start.1) | copy-done | bytes 294936
  32.4 0.0 copy-start.4
  32.4 0.7 copy-done.4
  33.1 20.0 %pairs.3 = (f32[32,384]{1,0:T(8,128)S(1)}, f32[16,4,384]{2,1,0:T(4,128)S(1)}) custom-call(s32[24,128]{1,0:T(8,128)S(1)} %copy-done.4, f32[32,1152]{1,0:T(8,128)S(1)} %copy-done, f32[16,4,1152]{2,1,0:T(4,128)S(1)} %copy-done.1), custom_call_target="tpu_custom_call" | custom-call | tf_op jit(solution)/shard_map/pairs/pallas_call | solution.py:520
  53.1 0.0 copy-start.2
  53.1 0.6 copy-done.2
  53.7 0.0 copy-start.3
  53.7 0.6 copy-done.3
  54.3 23.7 %reactions.1.pair_force = f32[32,384]{1,0:T(8,128)} custom-call(f32[32,384]{1,0:T(8,128)} %copy-done.3, f32[16,4,384]{2,1,0:T(4,128)} %copy-done.2, s32[128,128]{1,0:T(8,128)} %get-tuple-element.20.asked), custom_call_target="tpu_custom_call" | custom-call | tf_op jit(solution)/shard_map/reactions/pallas_call | solution.py:537
  78.0 2.9 %nodes.1 = f32[3,4096]{1,0:T(4,128)} custom-call(f32[32,384]{1,0:T(8,128)} %reactions.1.pair_force, f32[32,1152]{1,0:T(8,128)} %get-tuple-element.16.data, s32[2,4096]{1,0:T(2,128)} %conn.3, f32[3,3]{1,0:T(4,128)} %stress.1), custom_call_target="tpu_custom_call" | custom-call | tf_op jit(solution)/shard_map/nodes/pallas_call | solution.py:551
Async XLA Ops:
  7.4 24.0 %copy-start = (f32[32,1152]{1,0:T(8,128)S(1)}, f32[32,1152]{1,0:T(8,128)}, u32[]{:S(2)}) copy-start(f32[32,1152]{1,0:T(8,128)} %get-tuple-element.16.data) | copy-start | bytes 442372
  31.4 1.0 %copy-start.1 = (f32[16,4,1152]{2,1,0:T(4,128)S(1)}, f32[16,4,1152]{2,1,0:T(4,128)}, u32[]{:S(2)}) copy-start(f32[16,4,1152]{2,1,0:T(4,128)} %get-tuple-element.17.ghost) | copy-start | bytes 884740
  32.4 0.7 copy-start.4
  53.1 0.6 copy-start.2
  53.7 0.6 copy-start.3

commit v2 on v1

--- a/solution.py
+++ b/solution.py
@@ -8,9 +8,13 @@
 from jax.sharding import PartitionSpec as P
 
 SEG = 128
-COMPS = 9
+COMPS = 7
 ROWS = 16
-UNROLL = 4
+UNROLL = 8
+MIB = 1024 * 1024
+EXCHANGE_VMEM = 24 * MIB
+PAIRS_VMEM = 24 * MIB
+FINISH_VMEM = 16 * MIB
 MU_FACTOR = 10.0
 CORE_SQUARED = 0.25
 HALF_ROOT = 0.5**0.5
@@ -43,8 +47,8 @@
     return pieces
 
 
-def prep_kernel(pos, conn, burg, req, data, table, reqb, links):
-    blocks = data.shape[0]
+def segment_values(pos, conn, burg, links):
+    blocks = links.shape[1]
     for end in range(2):
         for b in range(blocks):
             links[end, b : b + 1, :] = conn[end : end + 1, b * SEG : (b + 1) * SEG]
@@ -63,59 +67,77 @@
         return tuple(out)
 
     zero = jnp.zeros((blocks, SEG), F32)
-    ends = lax.fori_loop(0, pos.shape[1] // SEG, step, (zero,) * 6)
-    comps = [0.5 * (ends[c] + ends[3 + c]) for c in range(3)]
-    comps += [ends[3 + c] - ends[c] for c in range(3)]
+    ends = lax.fori_loop(0, pos.shape[1] // SEG, step, (zero,) * 6, unroll=2)
+    values = [0.5 * (ends[c] + ends[3 + c]) for c in range(3)]
+    values += [ends[3 + c] - ends[c] for c in range(3)]
     diagonal = iota((blocks, blocks), 0) == iota((blocks, blocks), 1)
-    spread = jnp.where(diagonal, jnp.broadcast_to(burg[...], (blocks, blocks)), 0)
-    kind = jnp.broadcast_to(jnp.sum(spread, axis=1, keepdims=True), (blocks, SEG))
-    odd = jnp.where((kind & 1) == 1, -HALF_ROOT, HALF_ROOT)
-    comps.append(jnp.where(kind < 4, HALF_ROOT, 0.0))
-    comps.append(jnp.where(kind < 2, odd, jnp.where(kind < 4, 0.0, HALF_ROOT)))
-    comps.append(jnp.where(kind < 2, 0.0, odd))
-    table[...] = jnp.zeros(table.shape, table.dtype)
-    for c in range(COMPS):
-        lanes = slice(c * SEG, (c + 1) * SEG)
-        data[:, lanes] = comps[c]
-        for part, piece in enumerate(split(comps[c], 3)):
-            table[part * blocks : (part + 1) * blocks, lanes] = piece
+    kinds = jnp.broadcast_to(burg[...], (blocks, blocks)).astype(F32)
+    kind = jnp.sum(jnp.where(diagonal, kinds, 0.0), axis=1, keepdims=True)
+    values.append(jnp.broadcast_to(kind, (blocks, SEG)))
+    return values
+
+
+def burgers_of(kind):
+    odd = jnp.where((kind == 1.0) | (kind == 3.0) | (kind == 5.0), -HALF_ROOT, HALF_ROOT)
+    return [
+        jnp.where(kind < 4.0, HALF_ROOT, 0.0),
+        jnp.where(kind < 2.0, odd, jnp.where(kind < 4.0, 0.0, HALF_ROOT)),
+        jnp.where(kind < 2.0, 0.0, odd),
+    ]
+
+
+def fill_requests(req, reqb):
+    cap, owners = req.shape
     reqb[...] = jnp.full(reqb.shape, -1, I32)
-    owners, cap = req.shape
+    diagonal = iota((owners, owners), 0) == iota((owners, owners), 1)
     for t in range(cap):
-        reqb[pl.ds(t, owners, stride=8), :] = jnp.broadcast_to(req[:, t : t + 1], (owners, SEG))
+        row = jnp.broadcast_to(req[t : t + 1, :], (owners, owners)).astype(F32)
+        column = jnp.sum(jnp.where(diagonal, row, 0.0), axis=1, keepdims=True)
+        reqb[pl.ds(t, owners, stride=8), :] = jnp.broadcast_to(column, (owners, SEG)).astype(I32)
+
+
+def spread_columns(flat, columns):
+    blocks = columns.shape[0]
+
+    def step(block, carry):
+        tall = jnp.transpose(flat[pl.ds(pl.multiple_of(block * 8, 8), 8), :])
+        for c in range(6):
+            columns[block, c] = jnp.broadcast_to(tall[:, c : c + 1], (SEG, SEG))
+        return carry
+
+    lax.fori_loop(0, blocks, step, 0, unroll=2)
+
+
+def for_partners(me, rho, groups, cuts, run):
+    def step(i, carry):
+        hop = jnp.where(lax.rem(i, 2) == 0, groups // 2 + lax.div(i, 2), groups // 2 - lax.div(i + 1, 2))
+        m = lax.rem(lax.div(me, cuts) + hop, groups)
+        other = m * cuts + rho
+
+        @pl.when(other != me)
+        def _():
+            run(m, other)
+
+        return carry
+
+    lax.fori_loop(0, groups, step, 0)
 
 
 def greet(me, cut, rho, groups, cuts):
     barrier = pltpu.get_barrier_semaphore()
 
-    def step(m, carry):
-        other = m * cuts + rho
-
-        @pl.when(other != me)
-        def _():
-            pl.semaphore_signal(barrier, inc=1, device_id=(other, cut), device_id_type=MESH)
-
-        return carry
-
-    lax.fori_loop(0, groups, step, 0)
+    def signal(m, other):
+        pl.semaphore_signal(barrier, inc=1, device_id=(other, cut), device_id_type=MESH)
+
+    for_partners(me, rho, groups, cuts, signal)
     for d in range(1, cuts):
         peer = lax.rem(cut + d, cuts)
         pl.semaphore_signal(barrier, inc=1, device_id=(me, peer), device_id_type=MESH)
+
+
+def await_greetings(me, rho, groups, cuts):
     own = jnp.where(rho == lax.rem(me, cuts), 1, 0)
-    pl.semaphore_wait(barrier, groups + cuts - 1 - own)
-
-
-def for_partners(me, rho, groups, cuts, run):
-    def step(m, carry):
-        other = m * cuts + rho
-
-        @pl.when(other != me)
-        def _():
-            run(m, other)
-
-        return carry
-
-    lax.fori_loop(0, groups, step, 0)
+    pl.semaphore_wait(pltpu.get_barrier_semaphore(), groups + cuts - 1 - own)
 
 
 def prefix(flags):
@@ -189,9 +211,9 @@
 
 def exchange_kernel(
     cuts, groups, cap, blocks,
-    reqb, table, pairs,
-    ghost, asked, codes,
-    plist, stage, ordered, rsend, rrecv, psend, precv, bsend, brecv,
+    pos, conn, burg, req, pairs,
+    data, ghost, asked, codes, columns,
+    links, flat, reqb, table, plist, stage, ordered, rsend, rrecv, psend, precv, bsend, brecv,
 ):
     me = lax.axis_index("cell")
     cut = lax.axis_index("cuts")
@@ -199,11 +221,13 @@
     slot = lax.div(me, cuts)
     asked[...] = jnp.full(asked.shape, -1, I32)
     ghost[...] = jnp.zeros(ghost.shape, F32)
+    greet(me, cut, rho, groups, cuts)
+    fill_requests(req, reqb)
     plist[cut] = jnp.zeros(plist.shape[1:], I32)
     for e in range(2):
         for r in range(2):
             plist[cut, 2 * e + r : 2 * e + r + 1, :] = pairs[e : e + 1, r * SEG : (r + 1) * SEG]
-    greet(me, cut, rho, groups, cuts)
+    await_greetings(me, rho, groups, cuts)
 
     def request_copy(m, other):
         return pltpu.make_async_remote_copy(
@@ -238,6 +262,14 @@
     for_partners(me, rho, groups, cuts, lambda m, other: request_copy(m, other).start())
     for d in range(1, cuts):
         pair_copy(d, cut).start()
+    values = segment_values(pos, conn, burg, links)
+    table[...] = jnp.zeros(table.shape, table.dtype)
+    for c in range(COMPS):
+        lanes = slice(c * SEG, (c + 1) * SEG)
+        data[:, lanes] = values[c]
+        flat[pl.ds(c, blocks, stride=8), :] = values[c]
+        for part, piece in enumerate(split(values[c], 3)):
+            table[part * blocks : (part + 1) * blocks, lanes] = piece
     for_partners(me, rho, groups, cuts, lambda m, other: request_arrival(m, other).wait_recv())
 
     wide = asked.shape[0]
@@ -261,6 +293,7 @@
         )
 
     for_partners(me, rho, groups, cuts, lambda m, other: block_copy(m, other, slot).start())
+    spread_columns(flat, columns)
     for d in range(1, cuts):
         pair_copy(d, lax.rem(cut - d + cuts, cuts)).wait_recv()
     for j in range(cuts):
@@ -277,10 +310,9 @@
         pair_copy(d, cut).wait_send()
 
 
-def pair_kernel(codes, data, ghost, near_force, far_force, everything, total, moments, columns):
+def pair_kernel(codes, data, ghost, columns, near_force, far_force, everything, total, moments):
     blocks = data.shape[0]
     groups, cap, _ = ghost.shape
-    count_all = blocks + groups * cap
 
     def fill(target, row, value, start, rows):
         target[pl.ds(start * ROWS + row, rows, stride=ROWS), :] = value
@@ -290,29 +322,20 @@
             for part, piece in enumerate(split(values[c], 3)):
                 fill(moments, part * 3 + c, piece.astype(F32), start, rows)
 
+    def tile(ref, block, rows):
+        return ref[pl.ds(pl.multiple_of(block * ROWS, ROWS), rows), :]
+
+    def fill_block(values, start):
+        rows = values[0].shape[0]
+        for c, value in enumerate(values[:6] + burgers_of(values[6])):
+            fill(everything, c, value, start, rows)
+        fill_moments(values, start, rows)
+
     moments[...] = jnp.where((iota(moments.shape, 0) & (ROWS - 1)) == 9, 1.0, 0.0)
     total[...] = jnp.zeros(total.shape, F32)
-    everything[...] = jnp.zeros(everything.shape, F32)
-    values = [data[:, c * SEG : (c + 1) * SEG] for c in range(COMPS)]
-    for c in range(COMPS):
-        fill(everything, c, values[c], 0, blocks)
-    fill_moments(values, 0, blocks)
+    fill_block([data[:, c * SEG : (c + 1) * SEG] for c in range(COMPS)], 0)
     for m in range(groups):
-        values = [ghost[m, :, c * SEG : (c + 1) * SEG] for c in range(COMPS)]
-        for c in range(COMPS):
-            fill(everything, c, values[c], blocks + m * cap, cap)
-        fill_moments(values, blocks + m * cap, cap)
-
-    def tile(ref, block, rows):
-        return ref[pl.ds(pl.multiple_of(block * ROWS, ROWS), rows), :]
-
-    def spread(block, carry):
-        turned = jnp.transpose(tile(everything, block, 8))
-        for c in range(6):
-            columns[block, c] = jnp.broadcast_to(turned[:, c : c + 1], (SEG, SEG))
-        return carry
-
-    lax.fori_loop(0, blocks, spread, 0)
+        fill_block([ghost[m, :, c * SEG : (c + 1) * SEG] for c in range(COMPS)], blocks + m * cap)
 
     def one_pair(index):
         code = codes[index >> 7, index & (SEG - 1)]
@@ -384,19 +407,32 @@
             far_force[m, :, lanes] = force(blocks + m * cap, cap, c)
 
 
-def return_kernel(
+def finish_kernel(
     cuts, groups, cap, blocks,
-    near_force, far_force, asked,
-    result,
-    back, table, shares, bsend, brecv, ssend, srecv,
+    near_force, far_force, asked, data, conn, stress,
+    velocity,
+    back, table, shares, chosen, pieces, base, bsend, brecv, ssend, srecv,
 ):
     me = lax.axis_index("cell")
     cut = lax.axis_index("cuts")
     rho = lax.rem(cut - lax.rem(me, cuts) + cuts, cuts)
     slot = lax.div(me, cuts)
     back[...] = jnp.zeros(back.shape, F32)
+    greet(me, cut, rho, groups, cuts)
     table[...] = jnp.zeros(table.shape, F32)
-    greet(me, cut, rho, groups, cuts)
+
+    def node_of(b, end):
+        return conn[end : end + 1, pl.ds(pl.multiple_of(b * SEG, SEG), SEG)]
+
+    def choose(b, carry):
+        for end in range(2):
+            low = jnp.broadcast_to(node_of(b, end) & (SEG - 1), (SEG, SEG))
+            hit = iota((SEG, SEG), 0) == low
+            chosen[b, :, end * SEG : (end + 1) * SEG] = jnp.where(hit, 1.0, 0.0).astype(BF16)
+        return carry
+
+    lax.fori_loop(0, blocks, choose, 0, unroll=2)
+    await_greetings(me, rho, groups, cuts)
 
     def reaction_copy(m, other, at):
         return pltpu.make_async_remote_copy(
@@ -409,6 +445,44 @@
         )
 
     for_partners(me, rho, groups, cuts, lambda m, other: reaction_copy(m, other, slot).start())
+
+    def node_sums(first, last):
+        def step(g, carry):
+            at = pl.ds(pl.multiple_of(g * 8, 8), 8)
+            eight = [pieces[p, at, :] for p in range(first, last)]
+            for i in range(8):
+                b = g * 8 + i
+                left = []
+                for end in range(2):
+                    high = jnp.broadcast_to(node_of(b, end) >> 7, (blocks, SEG))
+                    hit = iota((blocks, SEG), 0) == high
+                    column = [
+                        jnp.where(hit, jnp.broadcast_to(piece[i : i + 1, :], (blocks, SEG)), 0.0)
+                        for piece in eight
+                    ]
+                    left.append(jnp.concatenate(column, axis=0).astype(BF16))
+                carry = carry + dot(jnp.concatenate(left, axis=1), chosen[b], NT)
+            return carry
+
+        start = jnp.zeros(((last - first) * blocks, SEG), F32)
+        sums = lax.fori_loop(0, blocks // 8, step, start)
+        rows = [sums[p * blocks : (p + 1) * blocks] for p in range(last - first)]
+        return [rows[p] + rows[p + 1] for p in range(0, last - first, 2)]
+
+    def set_piece(at, value):
+        for part, piece in enumerate(split(value, 2)):
+            pieces[at + part] = piece.astype(F32)
+
+    value = [data[:, c * SEG : (c + 1) * SEG] for c in range(COMPS)]
+    line = value[3:6]
+    burgers = burgers_of(value[6])
+    sigma = [[0.5 * (stress[a, b] + stress[b, a]) for b in range(3)] for a in range(3)]
+    pull = [sigma[a][0] * burgers[0] + sigma[a][1] * burgers[1] + sigma[a][2] * burgers[2] for a in range(3)]
+    for c in range(3):
+        u, v = (c + 1) % 3, (c + 2) % 3
+        base[:, c * SEG : (c + 1) * SEG] = pull[u] * line[v] - pull[v] * line[u]
+    set_piece(6, jnp.sqrt(line[0] * line[0] + line[1] * line[1] + line[2] * line[2] + CORE_SQUARED))
+    drag = node_sums(6, 8)[0]
     wide = asked.shape[0]
     hit = iota((wide, SEG), 1) == asked[...]
     onehot = jnp.transpose(jnp.where(hit, 1.0, 0.0))[:blocks, :].astype(BF16)
@@ -434,48 +508,19 @@
         share_copy(d, cut).start()
     for d in range(1, cuts):
         share_copy(d, lax.rem(cut - d + cuts, cuts)).wait_recv()
-    added = shares[0]
-    for j in range(1, cuts):
+    added = base[...]
+    for j in range(cuts):
         added = added + shares[j]
-    result[...] = added
+    for c in range(3):
+        set_piece(2 * c, added[:, c * SEG : (c + 1) * SEG])
+    sums = node_sums(0, 6)
+    for c in range(3):
+        speed = sums[c] / drag
+        for b in range(blocks):
+            velocity[c : c + 1, b * SEG : (b + 1) * SEG] = speed[b : b + 1, :]
     for d in range(1, cuts):
         share_copy(d, cut).wait_send()
     for_partners(me, rho, groups, cuts, lambda m, other: reaction_copy(m, other, m).wait_send())
-
-
-def node_kernel(pair_force, data, conn, stress, velocity):
-    blocks = data.shape[0]
-    value = [data[:, c * SEG : (c + 1) * SEG] for c in range(COMPS)]
-    line = value[3:6]
-    burgers = value[6:9]
-    sigma = [[0.5 * (stress[a, b] + stress[b, a]) for b in range(3)] for a in range(3)]
-    pull = [sigma[a][0] * burgers[0] + sigma[a][1] * burgers[1] + sigma[a][2] * burgers[2] for a in range(3)]
-    fields = []
-    for c in range(3):
-        u, v = (c + 1) % 3, (c + 2) % 3
-        turned = pull[u] * line[v] - pull[v] * line[u]
-        fields.append(pair_force[:, c * SEG : (c + 1) * SEG] + turned)
-    fields.append(jnp.sqrt(line[0] * line[0] + line[1] * line[1] + line[2] * line[2] + CORE_SQUARED))
-    pieces = [piece for field in fields for piece in split(field, 2)]
-    sums = jnp.zeros((len(pieces) * blocks, SEG), F32)
-    for b in range(blocks):
-        left, right = [], []
-        for end in range(2):
-            node = conn[end : end + 1, b * SEG : (b + 1) * SEG]
-            hit = iota((blocks, SEG), 0) == jnp.broadcast_to(node >> 7, (blocks, SEG))
-            column = [
-                jnp.where(hit, jnp.broadcast_to(piece[b : b + 1, :].astype(F32), (blocks, SEG)), 0.0)
-                for piece in pieces
-            ]
-            left.append(jnp.concatenate(column, axis=0).astype(BF16))
-            chosen = iota((SEG, SEG), 0) == jnp.broadcast_to(node & (SEG - 1), (SEG, SEG))
-            right.append(jnp.where(chosen, 1.0, 0.0).astype(BF16))
-        sums = sums + dot(jnp.concatenate(left, axis=1), jnp.concatenate(right, axis=1), NT)
-    merged = [sums[2 * f * blocks : (2 * f + 1) * blocks] + sums[(2 * f + 1) * blocks : (2 * f + 2) * blocks] for f in range(4)]
-    for c in range(3):
-        speed = merged[c] / merged[3]
-        for b in range(blocks):
-            velocity[c : c + 1, b * SEG : (b + 1) * SEG] = speed[b : b + 1, :]
 
 
 def body(cuts, node_positions, connectivity, burgers_index, applied_stress, ghost_request, pair_list):
@@ -485,76 +530,75 @@
     nodes = node_positions.shape[1]
     width = COMPS * SEG
     shape = jax.ShapeDtypeStruct
-    data, table, reqb = pl.pallas_call(
-        prep_kernel,
-        name="segments",
-        out_shape=(
-            shape((blocks, width), F32),
-            shape((SEG, width), BF16),
-            shape((owners * 8, SEG), I32),
-        ),
-        in_specs=[VMEM] * 4,
-        out_specs=(VMEM,) * 3,
-        scratch_shapes=[pltpu.VMEM((2, blocks, SEG), I32)],
-    )(node_positions, connectivity, burgers_index.reshape(1, blocks), ghost_request[0])
     dma = pltpu.SemaphoreType.DMA
-    ghost, asked, codes = pl.pallas_call(
+    data, ghost, asked, codes, columns = pl.pallas_call(
         functools.partial(exchange_kernel, cuts, groups, cap, blocks),
         name="exchange",
         out_shape=(
+            shape((blocks, width), F32),
             shape((groups, cap, width), F32),
             shape((groups * 8, SEG), I32),
             shape((24, SEG), I32),
+            shape((blocks, 6, SEG, SEG), F32),
         ),
-        in_specs=[VMEM] * 3,
-        out_specs=(VMEM,) * 3,
+        in_specs=[VMEM] * 5,
+        out_specs=(VMEM,) * 5,
         scratch_shapes=[
+            pltpu.VMEM((2, blocks, SEG), I32),
+            pltpu.VMEM((blocks * 8, SEG), F32),
+            pltpu.VMEM((owners * 8, SEG), I32),
+            pltpu.VMEM((SEG, width), BF16),
             pltpu.VMEM((cuts, 8, SEG), I32),
             pltpu.VMEM((groups, cap, width), F32),
             pltpu.VMEM((2, 8, SEG), I32),
             dma((groups,)), dma((groups,)), dma((cuts,)), dma((cuts,)), dma((groups,)), dma((groups,)),
         ],
-        compiler_params=pltpu.CompilerParams(collective_id=0, has_side_effects=True),
-    )(reqb, table, pair_list)
-    total_blocks = blocks + groups * cap
-    near_force, far_force = pl.pallas_call(
-        pair_kernel,
-        name="pairs",
-        out_shape=(
-            shape((blocks, 3 * SEG), F32),
-            shape((groups, cap, 3 * SEG), F32),
+        compiler_params=pltpu.CompilerParams(
+            collective_id=0, has_side_effects=True, vmem_limit_bytes=EXCHANGE_VMEM
         ),
-        in_specs=[SMEM, VMEM, VMEM],
-        out_specs=(VMEM,) * 2,
-        scratch_shapes=[
-            pltpu.VMEM((total_blocks * ROWS, SEG), F32),
-            pltpu.VMEM((total_blocks * ROWS, SEG), F32),
-            pltpu.VMEM((total_blocks * ROWS, SEG), F32),
-            pltpu.VMEM((blocks, 6, SEG, SEG), F32),
-        ],
-        compiler_params=pltpu.CompilerParams(vmem_limit_bytes=32 * 1024 * 1024),
-    )(codes, data, ghost)
-    pair_force = pl.pallas_call(
-        functools.partial(return_kernel, cuts, groups, cap, blocks),
-        name="reactions",
-        out_shape=shape((blocks, 3 * SEG), F32),
-        in_specs=[VMEM] * 3,
+    )(
+        node_positions,
+        connectivity,
+        burgers_index.reshape(1, blocks),
+        jnp.transpose(ghost_request[0]),
+        pair_list,
+    )
+    near_force, far_force = run_pairs(codes, data, ghost, columns)
+    return pl.pallas_call(
+        functools.partial(finish_kernel, cuts, groups, cap, blocks),
+        name="finish",
+        out_shape=shape((3, nodes), F32),
+        in_specs=[VMEM] * 5 + [SMEM],
         out_specs=VMEM,
         scratch_shapes=[
             pltpu.VMEM((groups, cap, 3 * SEG), F32),
             pltpu.VMEM((groups * 8, 3 * SEG), F32),
             pltpu.VMEM((cuts, blocks, 3 * SEG), F32),
+            pltpu.VMEM((blocks, SEG, 2 * SEG), BF16),
+            pltpu.VMEM((8, blocks, SEG), F32),
+            pltpu.VMEM((blocks, 3 * SEG), F32),
             dma((groups,)), dma((groups,)), dma((cuts,)), dma((cuts,)),
         ],
-        compiler_params=pltpu.CompilerParams(collective_id=1, has_side_effects=True),
-    )(near_force, far_force, asked)
+        compiler_params=pltpu.CompilerParams(
+            collective_id=1, has_side_effects=True, vmem_limit_bytes=FINISH_VMEM
+        ),
+    )(near_force, far_force, asked, data, connectivity, applied_stress)
+
+
+def run_pairs(codes, data, ghost, columns):
+    groups, cap, _ = ghost.shape
+    blocks = data.shape[0]
+    shape = jax.ShapeDtypeStruct
+    total_blocks = blocks + groups * cap
     return pl.pallas_call(
-        node_kernel,
-        name="nodes",
-        out_shape=shape((3, nodes), F32),
-        in_specs=[VMEM, VMEM, VMEM, SMEM],
-        out_specs=VMEM,
-    )(pair_force, data, connectivity, applied_stress)
+        pair_kernel,
+        name="pairs",
+        out_shape=(shape((blocks, 3 * SEG), F32), shape((groups, cap, 3 * SEG), F32)),
+        in_specs=[SMEM, VMEM, VMEM, VMEM],
+        out_specs=(VMEM,) * 2,
+        scratch_shapes=[pltpu.VMEM((total_blocks * ROWS, SEG), F32)] * 3,
+        compiler_params=pltpu.CompilerParams(vmem_limit_bytes=PAIRS_VMEM),
+    )(codes, data, ghost, columns)
 
 
 def solution(mesh):

time: 81.2 us -> 58.4 us (0.72)
  Pallas kernels: 76.5 us -> 53.8 us
    pallas_call x4 -> x2, Pallas kernels: 52.5 us -> 30.7 us  [the longest x1 22 us: body(): pl.pallas_call(functools.partial(finish_kernel, cuts, groups, cap, blocks...]
    pallas_call x1, Pallas kernels: 24 us -> 23.2 us  [body(): pl.pallas_call(functools.partial(exchange_kernel, cuts, groups, cap, bloc...]
    unnamed x11 -> x13, local copies, waits for them, and re-layouts: 4.29 us -> 4.26 us
where the time goes in v2:
time: 58.4 us; the launch traced here: 58.1 us
  Pallas kernels  53.8 us (92%)
  local copies, waits for them, and re-layouts  4.26 us (7%)
    pallas_call x1, Pallas kernels, body(): pl.pallas_call(functools.partial(exchange_kernel, cuts, groups, cap, bloc...  23.2 us
    pallas_call x1, Pallas kernels, body(): pl.pallas_call(functools.partial(finish_kernel, cuts, groups, cap, blocks...  22 us
    pallas_call x1, Pallas kernels, run_pairs(): pl.pallas_call(pair_kernel, name='pairs', out_shape=(shape((blocks, 3 * S...  8.63 us
    unnamed x13, local copies, waits for them, and re-layouts  4.26 us

profile of v2, /device:TPU:1, one launch (start us, length us, event | category | flops | bytes accessed | tf_op | source)
XLA Modules:
  0.0 58.1 jit_solution(1764315581155385817)
XLA Ops:
  0.0 0.0 copy-start.2
  0.0 0.0 copy-start
  0.0 0.8 %copy-done = s32[2,4096]{1,0:T(2,128)S(1)} copy-done((s32[2,4096]{1,0:T(2,128)S(1)}, s32[2,4096]{1,0:T(2,128)}, u32[]{:S(2)}) %copy-start) | copy-done | bytes 32792
  0.8 0.0 copy-start.1
  0.8 0.8 %copy-done.1 = f32[3,4096]{1,0:T(4,128)S(1)} copy-done((f32[3,4096]{1,0:T(4,128)S(1)}, f32[3,4096]{1,0:T(4,128)}, u32[]{:S(2)}) %copy-start.1) | copy-done | bytes 49176
  1.6 0.0 copy-start.3
  1.6 0.7 %copy-done.3 = s32[1,64,4]{1,2,0:T(4,128)S(1)} copy-done((s32[1,64,4]{1,2,0:T(4,128)S(1)}, s32[1,64,4]{1,2,0:T(4,128)}, u32[]{:S(2)}) %copy-start.3) | copy-done | bytes 1048
  2.3 0.0 copy-start.4
  2.3 0.7 %copy-done.4 = s32[2,256]{1,0:T(2,128)S(1)} copy-done((s32[2,256]{1,0:T(2,128)S(1)}, s32[2,256]{1,0:T(2,128)}, u32[]{:S(2)}) %copy-start.4) | copy-done | bytes 2072
  3.0 0.0 copy-start.5
  3.0 0.7 %copy-done.5 = s32[32]{0:T(128)S(1)} copy-done((s32[32]{0:T(128)S(1)}, s32[32]{0:T(128)}, u32[]{:S(2)}) %copy-start.5) | copy-done | bytes 152
  3.6 23.2 %exchange.1 = (f32[32,896]{1,0:T(8,128)S(1)}, f32[16,4,896]{2,1,0:T(4,128)S(1)}, s32[128,128]{1,0:T(8,128)S(1)}, s32[24,128]{1,0:T(8,128)S(1)}, f32[32,6,128,128]{3,2,1,0:T(8,128)S(1)}) custom-call(f32[3,4096]{1,0:T(4,128)S(1)} %copy-done.1, s32[2,4096]{1,0:T(2,128)S(1)} %copy-done, s32[1,32]{1,0:T(1,128)S(1)} %bitcast.5, s32[4,64]{1,0:T(4,128)S(1)} %bitcast.4, ...), custom_call_target="tpu_custom_call" | custom-call | tf_op jit(solution)/shard_map/exchange/pallas_call | solution.py:534
  26.8 8.6 %pairs.3 = (f32[32,384]{1,0:T(8,128)S(1)}, f32[16,4,384]{2,1,0:T(4,128)S(1)}) custom-call(s32[24,128]{1,0:T(8,128)S(1)} %get-tuple-element.12.codes, f32[32,896]{1,0:T(8,128)S(1)} %get-tuple-element.13.data, f32[16,4,896]{2,1,0:T(4,128)S(1)} %get-tuple-element.14.ghost, f32[32,6,128,128]{3,2,1,0:T(8,128)S(1)} %get-tuple-element.15.columns), custom_call_target="tpu_custom_call" | custom-call | tf_op jit(solution)/shard_map/pairs/pallas_call | solution.py:593
  35.4 0.0 copy-done.2
  35.4 22.0 %finish.1 = f32[3,4096]{1,0:T(4,128)S(1)} custom-call(f32[32,384]{1,0:T(8,128)S(1)} %get-tuple-element.16.near_force, f32[16,4,384]{2,1,0:T(4,128)S(1)} %get-tuple-element.17.far_force, s32[128,128]{1,0:T(8,128)S(1)} %get-tuple-element.18.asked, f32[32,896]{1,0:T(8,128)S(1)} %get-tuple-element.13.data, s32[2,4096]{1,0:T(2,128)S(1)} %copy-done, ...), custom_call_target="tpu_custom_call" | custom-call | tf_op jit(solution)/shard_map/finish/pallas_call | solution.py:567
  57.5 0.6 %copy.8 = f32[3,4096]{1,0:T(4,128)} copy(f32[3,4096]{1,0:T(4,128)S(1)} %finish.1) | data formatting | bytes 98304
Async XLA Ops:
  0.0 35.4 %copy-start.2 = (f32[3,3]{1,0:T(4,128)S(1)}, f32[3,3]{1,0:T(4,128)}, u32[]{:S(2)}) copy-start(f32[3,3]{1,0:T(4,128)} %stress.1) | copy-start | bytes 112
  0.0 0.8 %copy-start = (s32[2,4096]{1,0:T(2,128)S(1)}, s32[2,4096]{1,0:T(2,128)}, u32[]{:S(2)}) copy-start(s32[2,4096]{1,0:T(2,128)} %conn.3) | copy-start | bytes 98308
  0.8 0.8 %copy-start.1 = (f32[3,4096]{1,0:T(4,128)S(1)}, f32[3,4096]{1,0:T(4,128)}, u32[]{:S(2)}) copy-start(f32[3,4096]{1,0:T(4,128)} %pos.1) | copy-start | bytes 147460
  1.6 0.7 %copy-start.3 = (s32[1,64,4]{1,2,0:T(4,128)S(1)}, s32[1,64,4]{1,2,0:T(4,128)}, u32[]{:S(2)}) copy-start(s32[1,64,4]{1,2,0:T(4,128)} %param.10) | copy-start | bytes 3076
  2.3 0.7 %copy-start.4 = (s32[2,256]{1,0:T(2,128)S(1)}, s32[2,256]{1,0:T(2,128)}, u32[]{:S(2)}) copy-start(s32[2,256]{1,0:T(2,128)} %pairs.2) | copy-start | bytes 6148
  3.0 0.7 %copy-start.5 = (s32[32]{0:T(128)S(1)}, s32[32]{0:T(128)}, u32[]{:S(2)}) copy-start(s32[32]{0:T(128)} %param.8) | copy-start | bytes 388

commit v3 on v2

--- a/solution.py
+++ b/solution.py
@@ -9,6 +9,8 @@
 
 SEG = 128
 COMPS = 7
+SENT = 6
+FIRST_ASK = 64
 ROWS = 16
 UNROLL = 8
 MIB = 1024 * 1024
@@ -24,8 +26,13 @@
 I32 = jnp.int32
 VMEM = pl.BlockSpec(memory_space=pltpu.VMEM)
 SMEM = pl.BlockSpec(memory_space=pltpu.SMEM)
+ANY = pl.BlockSpec(memory_space=pltpu.HBM)
 NN = (((1,), (0,)), ((), ()))
 NT = (((1,), (1,)), ((), ()))
+
+
+def stay(value):
+    return pltpu.with_memory_space_constraint(value, pltpu.HBM)
 
 
 def iota(shape, axis):
@@ -78,22 +85,47 @@
 
 
 def burgers_of(kind):
-    odd = jnp.where((kind == 1.0) | (kind == 3.0) | (kind == 5.0), -HALF_ROOT, HALF_ROOT)
-    return [
-        jnp.where(kind < 4.0, HALF_ROOT, 0.0),
-        jnp.where(kind < 2.0, odd, jnp.where(kind < 4.0, 0.0, HALF_ROOT)),
-        jnp.where(kind < 2.0, 0.0, odd),
-    ]
-
-
-def fill_requests(req, reqb):
+    return [HALF_ROOT * value for value in whole_burgers(kind)]
+
+
+def fill_requests(req, burg, wide, rows):
     cap, owners = req.shape
-    reqb[...] = jnp.full(reqb.shape, -1, I32)
+    blocks = burg.shape[1]
+    wide[...] = jnp.zeros(wide.shape, I32)
+    wide[:, 0:blocks] = burg[...]
+    message = jnp.broadcast_to(wide[...], (owners, SEG))
+    lane = iota((owners, SEG), 1)
     diagonal = iota((owners, owners), 0) == iota((owners, owners), 1)
     for t in range(cap):
         row = jnp.broadcast_to(req[t : t + 1, :], (owners, owners)).astype(F32)
         column = jnp.sum(jnp.where(diagonal, row, 0.0), axis=1, keepdims=True)
-        reqb[pl.ds(t, owners, stride=8), :] = jnp.broadcast_to(column, (owners, SEG)).astype(I32)
+        column = jnp.broadcast_to(column, (owners, SEG)).astype(I32)
+        message = jnp.where(lane == FIRST_ASK + t, column, message)
+    for o in range(owners):
+        rows[o] = message[o : o + 1, :]
+
+
+def kind_table(own, heard, said, cap):
+    groups = heard.shape[0]
+    lane = iota((groups, SEG), 1)
+    blocks = FIRST_ASK // 2
+    wanted = jnp.zeros((groups, SEG), I32)
+    for t in range(cap):
+        column = jnp.broadcast_to(said[:, FIRST_ASK + t : FIRST_ASK + t + 1], (groups, SEG))
+        wanted = jnp.where((lane & 3) == t, column, wanted)
+    found = jnp.take_along_axis(heard, jnp.maximum(wanted, 0), axis=1)
+    here = (lane >= blocks) & (((lane - blocks) >> 2) == iota((groups, SEG), 0))
+    ghosts = jnp.sum(jnp.where(here, found, 0).astype(F32), axis=0, keepdims=True)
+    return jnp.where(iota((1, SEG), 1) < blocks, own.astype(F32), ghosts)
+
+
+def whole_burgers(kind):
+    odd = jnp.where((kind == 1.0) | (kind == 3.0) | (kind == 5.0), -1.0, 1.0)
+    return [
+        jnp.where(kind < 4.0, 1.0, 0.0),
+        jnp.where(kind < 2.0, odd, jnp.where(kind < 4.0, 0.0, 1.0)),
+        jnp.where(kind < 2.0, 0.0, odd),
+    ]
 
 
 def spread_columns(flat, columns):
@@ -160,8 +192,8 @@
     return jnp.sum(jnp.sum(value, axis=1, keepdims=True), axis=0, keepdims=True).astype(I32)
 
 
-def share_pairs(first, second, own_rows, me, cut, cuts, cap, blocks):
-    alive = first >= 0
+def share_pairs(first, second, own_row, kinds, me, cut, cuts, cap, blocks):
+    used = first >= 0
     ghost = second >= blocks
     slot = jnp.maximum(second - blocks, 0)
     owner = slot >> 2
@@ -170,27 +202,34 @@
     far = ghost & (owner != me)
     wanted = jnp.zeros_like(second)
     for t in range(cap):
-        row = jnp.broadcast_to(own_rows[t : t + 1, :], second.shape)
+        row = jnp.broadcast_to(own_row[:, FIRST_ASK + t : FIRST_ASK + t + 1], second.shape)
         wanted = jnp.where(part == t, row, wanted)
     near_block = jnp.where(own, wanted, second)
     block = jnp.where(far, blocks + (owner >> 2) * cap + part, near_block)
     half = jnp.logical_and(jnp.logical_not(far), block == first)
+    table = jnp.broadcast_to(kinds, first.shape)
+    one = whole_burgers(jnp.take_along_axis(table, jnp.maximum(first, 0), axis=1))
+    two = whole_burgers(jnp.take_along_axis(table, jnp.maximum(block, 0), axis=1))
+    match = one[0] * two[0] + one[1] * two[1] + one[2] * two[2]
+    match = jnp.where(half, 0.5 * match, match).astype(I32)
+    alive = used & (match != 0)
     place = (owner + me) & 3
     far_alive = alive & far
     near_alive = alive & jnp.logical_not(far)
-    target = (count(alive) + cuts - 1) >> 2
+    shares = [(count(used & far & (place == j)) * 53) >> 6 for j in range(cuts)]
+    target = (count(near_alive) + sum(shares) + cuts - 1) >> 2
     begin = jnp.zeros((1, 1), I32)
     low = begin
     top = begin
     for j in range(cuts):
-        room = jnp.maximum(target - count(far_alive & (place == j)), 0)
+        room = jnp.maximum(target - shares[j], 0)
         low = jnp.where(cut == j, begin, low)
         top = jnp.where(cut == j, begin + room, top)
         begin = begin + room
     rank = prefix(near_alive)
     mine = (far_alive & (place == cut)) | (near_alive & (rank >= low) & (rank < top))
     spot = prefix(mine)
-    first_code = jnp.where(mine, first + jnp.where(half, 64, 32), 0).astype(F32)
+    first_code = jnp.where(mine, first + 32 * (match + 2), 0).astype(F32)
     second_code = jnp.where(mine, block, 0).astype(F32)
     rows, lanes = first.shape
     codes = jnp.zeros((2 * rows, lanes), F32)
@@ -211,40 +250,37 @@
 
 def exchange_kernel(
     cuts, groups, cap, blocks,
-    pos, conn, burg, req, pairs,
+    pos_in, conn_in, burg_in, req_in, pairs_in,
     data, ghost, asked, codes, columns,
-    links, flat, reqb, table, plist, stage, ordered, rsend, rrecv, psend, precv, bsend, brecv,
+    pos, conn, burg, req, pairs, links, flat, wide, rows, heard, table, plist, stage, ordered,
+    isem, rsend, rrecv, psend, precv, bsend, brecv,
 ):
     me = lax.axis_index("cell")
     cut = lax.axis_index("cuts")
     rho = lax.rem(cut - lax.rem(me, cuts) + cuts, cuts)
     slot = lax.div(me, cuts)
-    asked[...] = jnp.full(asked.shape, -1, I32)
+    inputs = [(req_in, req), (burg_in, burg), (pairs_in, pairs), (conn_in, conn), (pos_in, pos)]
+    loads = [pltpu.make_async_copy(src, dst, isem.at[i]) for i, (src, dst) in enumerate(inputs)]
+    for load in loads:
+        load.start()
+    heard[...] = jnp.full(heard.shape, -1, I32)
     ghost[...] = jnp.zeros(ghost.shape, F32)
     greet(me, cut, rho, groups, cuts)
-    fill_requests(req, reqb)
+    for load in loads[:3]:
+        load.wait()
+    fill_requests(req, burg, wide, rows)
     plist[cut] = jnp.zeros(plist.shape[1:], I32)
     for e in range(2):
         for r in range(2):
             plist[cut, 2 * e + r : 2 * e + r + 1, :] = pairs[e : e + 1, r * SEG : (r + 1) * SEG]
     await_greetings(me, rho, groups, cuts)
 
-    def request_copy(m, other):
+    def request_copy(m, other, at):
         return pltpu.make_async_remote_copy(
-            src_ref=reqb.at[pl.ds(pl.multiple_of(other * 8, 8), 8)],
-            dst_ref=asked.at[pl.ds(pl.multiple_of(slot * 8, 8), 8)],
+            src_ref=rows.at[other],
+            dst_ref=heard.at[at],
             send_sem=rsend.at[m],
-            recv_sem=rrecv.at[slot],
-            device_id=(other, cut),
-            device_id_type=MESH,
-        )
-
-    def request_arrival(m, other):
-        return pltpu.make_async_remote_copy(
-            src_ref=reqb.at[pl.ds(pl.multiple_of(other * 8, 8), 8)],
-            dst_ref=asked.at[pl.ds(pl.multiple_of(m * 8, 8), 8)],
-            send_sem=rsend.at[m],
-            recv_sem=rrecv.at[m],
+            recv_sem=rrecv.at[at],
             device_id=(other, cut),
             device_id_type=MESH,
         )
@@ -259,24 +295,32 @@
             device_id_type=MESH,
         )
 
-    for_partners(me, rho, groups, cuts, lambda m, other: request_copy(m, other).start())
+    for_partners(me, rho, groups, cuts, lambda m, other: request_copy(m, other, slot).start())
     for d in range(1, cuts):
         pair_copy(d, cut).start()
+    for load in loads[3:]:
+        load.wait()
     values = segment_values(pos, conn, burg, links)
     table[...] = jnp.zeros(table.shape, table.dtype)
     for c in range(COMPS):
         lanes = slice(c * SEG, (c + 1) * SEG)
         data[:, lanes] = values[c]
+        if c == SENT:
+            continue
         flat[pl.ds(c, blocks, stride=8), :] = values[c]
         for part, piece in enumerate(split(values[c], 3)):
             table[part * blocks : (part + 1) * blocks, lanes] = piece
-    for_partners(me, rho, groups, cuts, lambda m, other: request_arrival(m, other).wait_recv())
-
-    wide = asked.shape[0]
-    lane = iota((wide, SEG), 1)
+    for_partners(me, rho, groups, cuts, lambda m, other: request_copy(m, other, m).wait_recv())
+    hear = jnp.concatenate([heard[m] for m in range(groups)], axis=0)
+    asked[...] = jnp.full(asked.shape, -1, I32)
+    for t in range(cap):
+        column = hear[:, FIRST_ASK + t : FIRST_ASK + t + 1]
+        asked[pl.ds(t, groups, stride=8), :] = jnp.broadcast_to(column, (groups, SEG))
+
+    lane = iota(asked.shape, 1)
     hit = ((lane & (blocks - 1)) == asked[...]) & (lane < 3 * blocks)
     onehot = jnp.where(hit, 1.0, 0.0).astype(BF16)
-    for c in range(COMPS):
+    for c in range(SENT):
         lanes = slice(c * SEG, (c + 1) * SEG)
         got = dot(onehot, table[:, lanes], NN)
         for m in range(groups):
@@ -299,13 +343,15 @@
     for j in range(cuts):
         ordered[0, 2 * j : 2 * j + 2, :] = plist[j, 0:2, :]
         ordered[1, 2 * j : 2 * j + 2, :] = plist[j, 2:4, :]
-    own_rows = reqb[pl.ds(pl.multiple_of(me * 8, 8), 8), :]
-    listed, total = share_pairs(ordered[0], ordered[1], own_rows, me, cut, cuts, cap, blocks)
+    said = jnp.concatenate([rows[m * cuts + rho] for m in range(groups)], axis=0)
+    own_row = rows[me]
+    kinds = kind_table(own_row, hear, said, cap)
+    listed, total = share_pairs(ordered[0], ordered[1], own_row, kinds, me, cut, cuts, cap, blocks)
     codes[0:16, :] = listed
     codes[16:24, :] = jnp.broadcast_to(total, (8, SEG))
     for_partners(me, rho, groups, cuts, lambda m, other: block_copy(m, other, m).wait_recv())
     for_partners(me, rho, groups, cuts, lambda m, other: block_copy(m, other, m).wait_send())
-    for_partners(me, rho, groups, cuts, lambda m, other: request_copy(m, other).wait_send())
+    for_partners(me, rho, groups, cuts, lambda m, other: request_copy(m, other, m).wait_send())
     for d in range(1, cuts):
         pair_copy(d, cut).wait_send()
 
@@ -327,26 +373,23 @@
 
     def fill_block(values, start):
         rows = values[0].shape[0]
-        for c, value in enumerate(values[:6] + burgers_of(values[6])):
+        for c, value in enumerate(values):
             fill(everything, c, value, start, rows)
         fill_moments(values, start, rows)
 
     moments[...] = jnp.where((iota(moments.shape, 0) & (ROWS - 1)) == 9, 1.0, 0.0)
     total[...] = jnp.zeros(total.shape, F32)
-    fill_block([data[:, c * SEG : (c + 1) * SEG] for c in range(COMPS)], 0)
+    fill_block([data[:, c * SEG : (c + 1) * SEG] for c in range(SENT)], 0)
     for m in range(groups):
-        fill_block([ghost[m, :, c * SEG : (c + 1) * SEG] for c in range(COMPS)], blocks + m * cap)
+        fill_block([ghost[m, :, c * SEG : (c + 1) * SEG] for c in range(SENT)], blocks + m * cap)
 
     def one_pair(index):
         code = codes[index >> 7, index & (SEG - 1)]
         second = codes[8 + (index >> 7), index & (SEG - 1)]
         first = code & 31
         kind = code >> 5
-        scale = jnp.where(kind == 1, MU_FACTOR, jnp.where(kind == 2, 0.5 * MU_FACTOR, 0.0))
-        near = tile(everything, first, ROWS)
+        factor = jnp.where(kind == 0, 0.0, (0.5 * MU_FACTOR) * (kind - 2).astype(F32))
         far = tile(everything, second, ROWS)
-        match = near[6:7] * far[6:7] + near[7:8] * far[7:8] + near[8:9] * far[8:9]
-        factor = match * scale
         middle = [far[c : c + 1] for c in range(3)]
         line = [far[3 + c : 4 + c] * factor for c in range(3)]
         high, low = [], []
@@ -409,14 +452,16 @@
 
 def finish_kernel(
     cuts, groups, cap, blocks,
-    near_force, far_force, asked, data, conn, stress,
+    near_force, far_force, asked, data, conn_in, stress,
     velocity,
-    back, table, shares, chosen, pieces, base, bsend, brecv, ssend, srecv,
+    conn, isem, back, table, shares, chosen, pieces, base, bsend, brecv, ssend, srecv,
 ):
     me = lax.axis_index("cell")
     cut = lax.axis_index("cuts")
     rho = lax.rem(cut - lax.rem(me, cuts) + cuts, cuts)
     slot = lax.div(me, cuts)
+    load = pltpu.make_async_copy(conn_in, conn, isem)
+    load.start()
     back[...] = jnp.zeros(back.shape, F32)
     greet(me, cut, rho, groups, cuts)
     table[...] = jnp.zeros(table.shape, F32)
@@ -431,6 +476,7 @@
             chosen[b, :, end * SEG : (end + 1) * SEG] = jnp.where(hit, 1.0, 0.0).astype(BF16)
         return carry
 
+    load.wait()
     lax.fori_loop(0, blocks, choose, 0, unroll=2)
     await_greetings(me, rho, groups, cuts)
 
@@ -483,8 +529,7 @@
         base[:, c * SEG : (c + 1) * SEG] = pull[u] * line[v] - pull[v] * line[u]
     set_piece(6, jnp.sqrt(line[0] * line[0] + line[1] * line[1] + line[2] * line[2] + CORE_SQUARED))
     drag = node_sums(6, 8)[0]
-    wide = asked.shape[0]
-    hit = iota((wide, SEG), 1) == asked[...]
+    hit = iota(asked.shape, 1) == asked[...]
     onehot = jnp.transpose(jnp.where(hit, 1.0, 0.0))[:blocks, :].astype(BF16)
     for_partners(me, rho, groups, cuts, lambda m, other: reaction_copy(m, other, m).wait_recv())
     for m in range(groups):
@@ -536,41 +581,51 @@
         name="exchange",
         out_shape=(
             shape((blocks, width), F32),
-            shape((groups, cap, width), F32),
+            shape((groups, cap, SENT * SEG), F32),
             shape((groups * 8, SEG), I32),
             shape((24, SEG), I32),
             shape((blocks, 6, SEG, SEG), F32),
         ),
-        in_specs=[VMEM] * 5,
+        in_specs=[ANY] * 5,
         out_specs=(VMEM,) * 5,
         scratch_shapes=[
+            pltpu.VMEM((3, nodes), F32),
+            pltpu.VMEM((2, nodes), I32),
+            pltpu.VMEM((1, blocks), I32),
+            pltpu.VMEM((cap, owners), I32),
+            pltpu.VMEM(pair_list.shape, I32),
             pltpu.VMEM((2, blocks, SEG), I32),
             pltpu.VMEM((blocks * 8, SEG), F32),
-            pltpu.VMEM((owners * 8, SEG), I32),
-            pltpu.VMEM((SEG, width), BF16),
+            pltpu.VMEM((1, SEG), I32),
+            pltpu.VMEM((owners, 1, SEG), I32),
+            pltpu.VMEM((groups, 1, SEG), I32),
+            pltpu.VMEM((SEG, SENT * SEG), BF16),
             pltpu.VMEM((cuts, 8, SEG), I32),
-            pltpu.VMEM((groups, cap, width), F32),
+            pltpu.VMEM((groups, cap, SENT * SEG), F32),
             pltpu.VMEM((2, 8, SEG), I32),
+            dma((5,)),
             dma((groups,)), dma((groups,)), dma((cuts,)), dma((cuts,)), dma((groups,)), dma((groups,)),
         ],
         compiler_params=pltpu.CompilerParams(
             collective_id=0, has_side_effects=True, vmem_limit_bytes=EXCHANGE_VMEM
         ),
     )(
-        node_positions,
-        connectivity,
-        burgers_index.reshape(1, blocks),
-        jnp.transpose(ghost_request[0]),
-        pair_list,
+        stay(node_positions),
+        stay(connectivity),
+        stay(burgers_index.reshape(1, blocks)),
+        stay(jnp.transpose(ghost_request[0])),
+        stay(pair_list),
     )
     near_force, far_force = run_pairs(codes, data, ghost, columns)
     return pl.pallas_call(
         functools.partial(finish_kernel, cuts, groups, cap, blocks),
         name="finish",
         out_shape=shape((3, nodes), F32),
-        in_specs=[VMEM] * 5 + [SMEM],
+        in_specs=[VMEM] * 4 + [ANY, SMEM],
         out_specs=VMEM,
         scratch_shapes=[
+            pltpu.VMEM((2, nodes), I32),
+            dma,
             pltpu.VMEM((groups, cap, 3 * SEG), F32),
             pltpu.VMEM((groups * 8, 3 * SEG), F32),
             pltpu.VMEM((cuts, blocks, 3 * SEG), F32),
@@ -582,7 +637,7 @@
         compiler_params=pltpu.CompilerParams(
             collective_id=1, has_side_effects=True, vmem_limit_bytes=FINISH_VMEM
         ),
-    )(near_force, far_force, asked, data, connectivity, applied_stress)
+    )(near_force, far_force, asked, data, stay(connectivity), applied_stress)
 
 
 def run_pairs(codes, data, ghost, columns):

time: 58.4 us -> 52 us (0.89)
  local copies, waits for them, and re-layouts: 4.26 us -> 0.64 us
  Pallas kernels: 53.8 us -> 51.2 us
    unnamed x13 -> x3, local copies, waits for them, and re-layouts: 4.26 us -> 0.64 us
    pallas_call x1, Pallas kernels: 22 us -> 18.8 us  [body(): pl.pallas_call(functools.partial(finish_kernel, cuts, groups, cap, blocks...]
    pallas_call x1, Pallas kernels: 8.63 us -> 9.41 us  [run_pairs(): pl.pallas_call(pair_kernel, name='pairs', out_shape=(shape((blocks, 3 * S...]
where the time goes in v3:
time: 52 us; the launch traced here: 51.8 us
  Pallas kernels  51.2 us (98%)
  local copies, waits for them, and re-layouts  0.64 us (1%)
    pallas_call x1, Pallas kernels, body(): pl.pallas_call(functools.partial(exchange_kernel, cuts, groups, cap, bloc...  22.9 us
    pallas_call x1, Pallas kernels, body(): pl.pallas_call(functools.partial(finish_kernel, cuts, groups, cap, blocks...  18.8 us
    pallas_call x1, Pallas kernels, run_pairs(): pl.pallas_call(pair_kernel, name='pairs', out_shape=(shape((blocks, 3 * S...  9.41 us

profile of v3, /device:TPU:1, one launch (start us, length us, event | category | flops | bytes accessed | tf_op | source)
XLA Modules:
  0.0 51.8 jit_solution(10197089553533208191)
XLA Ops:
  0.0 0.0 copy-start
  0.0 22.9 %exchange.1 = (f32[32,896]{1,0:T(8,128)S(1)}, f32[16,4,768]{2,1,0:T(4,128)S(1)}, s32[128,128]{1,0:T(8,128)S(1)}, s32[24,128]{1,0:T(8,128)S(1)}, f32[32,6,128,128]{3,2,1,0:T(8,128)S(1)}) custom-call(f32[3,4096]{1,0:T(4,128)} %pos_in.1, s32[2,4096]{1,0:T(2,128)} %conn_in.3, s32[1,32]{1,0:T(1,128)} %bitcast.5, s32[4,64]{1,0:T(4,128)} %bitcast.4, s32[2,256]{1,0:T(2,128)} %pairs_in.1), custom_call_target="tpu_custom_call" | custom-call | tf_op jit(solution)/shard_map/exchange/pallas_call | solution.py:579
  22.9 9.4 %pairs.1 = (f32[32,384]{1,0:T(8,128)S(1)}, f32[16,4,384]{2,1,0:T(4,128)S(1)}) custom-call(s32[24,128]{1,0:T(8,128)S(1)} %get-tuple-element.12.codes, f32[32,896]{1,0:T(8,128)S(1)} %get-tuple-element.13.data, f32[16,4,768]{2,1,0:T(4,128)S(1)} %get-tuple-element.14.ghost, f32[32,6,128,128]{3,2,1,0:T(8,128)S(1)} %get-tuple-element.15.columns), custom_call_target="tpu_custom_call" | custom-call | tf_op jit(solution)/shard_map/pairs/pallas_call | solution.py:648
  32.4 0.0 copy-done
  32.4 18.8 %finish.1 = f32[3,4096]{1,0:T(4,128)S(1)} custom-call(f32[32,384]{1,0:T(8,128)S(1)} %get-tuple-element.16.near_force, f32[16,4,384]{2,1,0:T(4,128)S(1)} %get-tuple-element.17.far_force, s32[128,128]{1,0:T(8,128)S(1)} %get-tuple-element.18.asked, f32[32,896]{1,0:T(8,128)S(1)} %get-tuple-element.13.data, s32[2,4096]{1,0:T(2,128)} %conn_in.3, f32[3,3]{1,0:T(4,128)S(1)} %copy-done), custom_call_target="tpu_custom_call" | custom-call | tf_op jit(solution)/shard_map/finish/pallas_call | solution.py:620
  51.2 0.6 %copy.8 = f32[3,4096]{1,0:T(4,128)} copy(f32[3,4096]{1,0:T(4,128)S(1)} %finish.1) | data formatting | bytes 98304
Async XLA Ops:
  0.0 32.4 %copy-start = (f32[3,3]{1,0:T(4,128)S(1)}, f32[3,3]{1,0:T(4,128)}, u32[]{:S(2)}) copy-start(f32[3,3]{1,0:T(4,128)} %stress.1) | copy-start | bytes 112

commit v4 on v3

--- a/solution.py
+++ b/solution.py
@@ -13,10 +13,15 @@
 FIRST_ASK = 64
 ROWS = 16
 UNROLL = 8
+FAR_SLOTS = 120
+NEAR_SLOTS = 40
+FAR_ROW = 8
+NEAR_ROW = 9
+LIST_ROWS = 16
 MIB = 1024 * 1024
 EXCHANGE_VMEM = 24 * MIB
 PAIRS_VMEM = 24 * MIB
-FINISH_VMEM = 16 * MIB
+FINISH_VMEM = 24 * MIB
 MU_FACTOR = 10.0
 CORE_SQUARED = 0.25
 HALF_ROOT = 0.5**0.5
@@ -214,44 +219,41 @@
     match = jnp.where(half, 0.5 * match, match).astype(I32)
     alive = used & (match != 0)
     place = (owner + me) & 3
-    far_alive = alive & far
-    near_alive = alive & jnp.logical_not(far)
-    shares = [(count(used & far & (place == j)) * 53) >> 6 for j in range(cuts)]
-    target = (count(near_alive) + sum(shares) + cuts - 1) >> 2
-    begin = jnp.zeros((1, 1), I32)
-    low = begin
-    top = begin
-    for j in range(cuts):
-        room = jnp.maximum(target - shares[j], 0)
-        low = jnp.where(cut == j, begin, low)
-        top = jnp.where(cut == j, begin + room, top)
-        begin = begin + room
-    rank = prefix(near_alive)
-    mine = (far_alive & (place == cut)) | (near_alive & (rank >= low) & (rank < top))
-    spot = prefix(mine)
+    mine_far = alive & far & (place == cut)
+    near = alive & jnp.logical_not(far)
+    part_size = (count(near) + cuts - 1) >> 2
+    rank = prefix(near) - cut * part_size
+    mine_near = near & (rank >= 0) & (rank < part_size)
+    far_spot = prefix(mine_far)
+    fits = (mine_far & (far_spot < FAR_SLOTS)) | (mine_near & (rank < NEAR_SLOTS))
+    mine = mine_far | mine_near
+    rest = mine & jnp.logical_not(fits)
+    lanes = first.shape[1]
+    spot = jnp.where(far, FAR_ROW * lanes + far_spot, NEAR_ROW * lanes + rank)
+    spot = jnp.where(fits, spot, prefix(rest))
     first_code = jnp.where(mine, first + 32 * (match + 2), 0).astype(F32)
     second_code = jnp.where(mine, block, 0).astype(F32)
-    rows, lanes = first.shape
-    codes = jnp.zeros((2 * rows, lanes), F32)
+    rows = first.shape[0]
+    codes = jnp.zeros((2 * LIST_ROWS, lanes), F32)
     for r in range(rows):
         at = spot[r : r + 1, :]
-        hit = iota((rows, lanes), 0) == jnp.broadcast_to(at >> 7, (rows, lanes))
+        hit = iota((LIST_ROWS, lanes), 0) == jnp.broadcast_to(at >> 7, (LIST_ROWS, lanes))
         left = jnp.concatenate(
             [
-                jnp.where(hit, jnp.broadcast_to(first_code[r : r + 1, :], (rows, lanes)), 0.0),
-                jnp.where(hit, jnp.broadcast_to(second_code[r : r + 1, :], (rows, lanes)), 0.0),
+                jnp.where(hit, jnp.broadcast_to(first_code[r : r + 1, :], (LIST_ROWS, lanes)), 0.0),
+                jnp.where(hit, jnp.broadcast_to(second_code[r : r + 1, :], (LIST_ROWS, lanes)), 0.0),
             ],
             axis=0,
         ).astype(BF16)
         chosen = iota((lanes, lanes), 0) == jnp.broadcast_to(at & (lanes - 1), (lanes, lanes))
         codes = codes + dot(left, jnp.where(chosen, 1.0, 0.0).astype(BF16), NT)
-    return codes.astype(I32), count(mine)
+    return codes.astype(I32), count(rest)
 
 
 def exchange_kernel(
     cuts, groups, cap, blocks,
     pos_in, conn_in, burg_in, req_in, pairs_in,
-    data, ghost, asked, codes, columns,
+    data, ghost, asked, codes, extra, columns,
     pos, conn, burg, req, pairs, links, flat, wide, rows, heard, table, plist, stage, ordered,
     isem, rsend, rrecv, psend, precv, bsend, brecv,
 ):
@@ -347,8 +349,8 @@
     own_row = rows[me]
     kinds = kind_table(own_row, hear, said, cap)
     listed, total = share_pairs(ordered[0], ordered[1], own_row, kinds, me, cut, cuts, cap, blocks)
-    codes[0:16, :] = listed
-    codes[16:24, :] = jnp.broadcast_to(total, (8, SEG))
+    codes[...] = listed
+    extra[...] = jnp.broadcast_to(total, extra.shape)
     for_partners(me, rho, groups, cuts, lambda m, other: block_copy(m, other, m).wait_recv())
     for_partners(me, rho, groups, cuts, lambda m, other: block_copy(m, other, m).wait_send())
     for_partners(me, rho, groups, cuts, lambda m, other: request_copy(m, other, m).wait_send())
@@ -356,105 +358,109 @@
         pair_copy(d, cut).wait_send()
 
 
-def pair_kernel(codes, data, ghost, columns, near_force, far_force, everything, total, moments):
+def fill_tables(data, ghost, everything, moments):
     blocks = data.shape[0]
     groups, cap, _ = ghost.shape
 
-    def fill(target, row, value, start, rows):
-        target[pl.ds(start * ROWS + row, rows, stride=ROWS), :] = value
-
-    def fill_moments(values, start, rows):
+    def fill(target, row, value, start):
+        target[start : start + value.shape[0], row, :] = value
+
+    def fill_block(values, start):
+        for c, value in enumerate(values):
+            fill(everything, c, value, start)
         for c in range(3):
             for part, piece in enumerate(split(values[c], 3)):
-                fill(moments, part * 3 + c, piece.astype(F32), start, rows)
-
-    def tile(ref, block, rows):
-        return ref[pl.ds(pl.multiple_of(block * ROWS, ROWS), rows), :]
-
-    def fill_block(values, start):
-        rows = values[0].shape[0]
-        for c, value in enumerate(values):
-            fill(everything, c, value, start, rows)
-        fill_moments(values, start, rows)
-
-    moments[...] = jnp.where((iota(moments.shape, 0) & (ROWS - 1)) == 9, 1.0, 0.0)
-    total[...] = jnp.zeros(total.shape, F32)
+                fill(moments, part * 3 + c, piece.astype(F32), start)
+
+    moments[...] = jnp.where(iota(moments.shape, 1) == 9, 1.0, 0.0)
     fill_block([data[:, c * SEG : (c + 1) * SEG] for c in range(SENT)], 0)
     for m in range(groups):
         fill_block([ghost[m, :, c * SEG : (c + 1) * SEG] for c in range(SENT)], blocks + m * cap)
 
-    def one_pair(index):
-        code = codes[index >> 7, index & (SEG - 1)]
-        second = codes[8 + (index >> 7), index & (SEG - 1)]
-        first = code & 31
-        kind = code >> 5
-        factor = jnp.where(kind == 0, 0.0, (0.5 * MU_FACTOR) * (kind - 2).astype(F32))
-        far = tile(everything, second, ROWS)
-        middle = [far[c : c + 1] for c in range(3)]
-        line = [far[3 + c : 4 + c] * factor for c in range(3)]
-        high, low = [], []
-        step = 32
-        for start in range(0, SEG, step):
-            rows = slice(start, start + step)
-            r = [columns[first, c, rows, :] - middle[c] for c in range(3)]
-            dist = r[0] * r[0] + CORE_SQUARED + r[1] * r[1] + r[2] * r[2]
-            g = (
-                columns[first, 3, rows, :] * line[0]
-                + columns[first, 4, rows, :] * line[1]
-                + columns[first, 5, rows, :] * line[2]
-            )
-            inverse = lax.rsqrt(dist)
-            weight = g * inverse * (inverse * inverse)
-            big, small = split(weight, 2)
-            high.append(big)
-            low.append(small)
-        high = jnp.concatenate(high, axis=0)
-        low = jnp.concatenate(low, axis=0)
-        near_moments = tile(moments, first, ROWS).astype(BF16)
-        far_moments = tile(moments, second, ROWS).astype(BF16)
-        on_first = dot(
-            jnp.concatenate([far_moments, far_moments], axis=1),
-            jnp.concatenate([high, low], axis=1),
-            NT,
+
+def one_pair(code, second, everything, moments, columns):
+    first = code & 31
+    kind = code >> 5
+    factor = jnp.where(kind == 0, 0.0, (0.5 * MU_FACTOR) * (kind - 2).astype(F32))
+    far = everything[second]
+    middle = [far[c : c + 1] for c in range(3)]
+    line = [far[3 + c : 4 + c] * factor for c in range(3)]
+    high, low = [], []
+    step = 32
+    for start in range(0, SEG, step):
+        rows = slice(start, start + step)
+        r = [columns[first, c, rows, :] - middle[c] for c in range(3)]
+        dist = r[0] * r[0] + CORE_SQUARED + r[1] * r[1] + r[2] * r[2]
+        g = (
+            columns[first, 3, rows, :] * line[0]
+            + columns[first, 4, rows, :] * line[1]
+            + columns[first, 5, rows, :] * line[2]
         )
-        on_second = dot(
-            jnp.concatenate([near_moments, near_moments], axis=1),
-            jnp.concatenate([high, low], axis=0),
-            NN,
-        )
-        return first, second, on_first, on_second
-
-    def body(step, carry):
-        results = [one_pair(step * UNROLL + u) for u in range(UNROLL)]
-        for first, second, on_first, on_second in results:
-            at = pl.ds(pl.multiple_of(first * ROWS, ROWS), ROWS)
-            total[at, :] = total[at, :] + on_first
-            at = pl.ds(pl.multiple_of(second * ROWS, ROWS), ROWS)
-            total[at, :] = total[at, :] + on_second
-        return carry
-
-    lax.fori_loop(0, (codes[16, 0] + UNROLL - 1) // UNROLL, body, 0)
-
-    def take(ref, row, start, rows):
-        return ref[pl.ds(start * ROWS + row, rows, stride=ROWS), :]
-
-    def force(start, rows, c):
-        weight = take(total, 9, start, rows)
-        others = take(total, c, start, rows) + take(total, 3 + c, start, rows) + take(total, 6 + c, start, rows)
-        return take(everything, c, start, rows) * weight - others
-
-    for c in range(3):
-        lanes = slice(c * SEG, (c + 1) * SEG)
-        near_force[:, lanes] = force(0, blocks, c)
-        for m in range(groups):
-            far_force[m, :, lanes] = force(blocks + m * cap, cap, c)
+        inverse = lax.rsqrt(dist)
+        big, small = split(g * inverse * (inverse * inverse), 2)
+        high.append(big)
+        low.append(small)
+    high = jnp.concatenate(high, axis=0)
+    low = jnp.concatenate(low, axis=0)
+    near_moments = moments[first].astype(BF16)
+    far_moments = moments[second].astype(BF16)
+    on_first = dot(
+        jnp.concatenate([far_moments, far_moments], axis=1),
+        jnp.concatenate([high, low], axis=1),
+        NT,
+    )
+    on_second = dot(
+        jnp.concatenate([near_moments, near_moments], axis=1),
+        jnp.concatenate([high, low], axis=0),
+        NN,
+    )
+    return first, on_first, on_second
+
+
+def extra_kernel(extra, codes_in, data, ghost, columns, near_force, far_force, codes, sem, everything, moments, total):
+    blocks = data.shape[0]
+    groups, cap, _ = ghost.shape
+    near_force[...] = jnp.zeros(near_force.shape, F32)
+    far_force[...] = jnp.zeros(far_force.shape, F32)
+
+    @pl.when(extra[0, 0] > 0)
+    def _():
+        load = pltpu.make_async_copy(codes_in, codes, sem)
+        load.start()
+        total[...] = jnp.zeros(total.shape, F32)
+        fill_tables(data, ghost, everything, moments)
+        load.wait()
+
+        def body(index, carry):
+            code = codes[index >> 7, index & (SEG - 1)]
+            second = codes[LIST_ROWS + (index >> 7), index & (SEG - 1)]
+            first, on_first, on_second = one_pair(code, second, everything, moments, columns)
+            total[first] = total[first] + on_first
+            total[second] = total[second] + on_second
+            return carry
+
+        lax.fori_loop(0, extra[0, 0], body, 0)
+
+        def take(ref, row, start, rows):
+            return ref[start : start + rows, row, :]
+
+        def force(start, rows, c):
+            weight = take(total, 9, start, rows)
+            others = sum(take(total, 3 * part + c, start, rows) for part in range(3))
+            return take(everything, c, start, rows) * weight - others
+
+        for c in range(3):
+            lanes = slice(c * SEG, (c + 1) * SEG)
+            near_force[:, lanes] = force(0, blocks, c)
+            for m in range(groups):
+                far_force[m, :, lanes] = force(blocks + m * cap, cap, c)
 
 
 def finish_kernel(
     cuts, groups, cap, blocks,
-    near_force, far_force, asked, data, conn_in, stress,
+    near_extra, far_extra, codes_in, asked, data, ghost, columns, conn_in, stress,
     velocity,
-    conn, isem, back, table, shares, chosen, pieces, base, bsend, brecv, ssend, srecv,
+    conn, isem, codes, csem, everything, moments, results, sums_of, near_force, far_force, back, table, shares, chosen, length, base, bsend, brecv, ssend, srecv,
 ):
     me = lax.axis_index("cell")
     cut = lax.axis_index("cuts")
@@ -462,9 +468,58 @@
     slot = lax.div(me, cuts)
     load = pltpu.make_async_copy(conn_in, conn, isem)
     load.start()
+    load_codes = pltpu.make_async_copy(codes_in, codes, csem)
+    load_codes.start()
     back[...] = jnp.zeros(back.shape, F32)
     greet(me, cut, rho, groups, cuts)
     table[...] = jnp.zeros(table.shape, F32)
+    fill_tables(data, ghost, everything, moments)
+    load_codes.wait()
+
+    def run_list(row, slots):
+        def step(i, carry):
+            for u in range(UNROLL):
+                at = i * UNROLL + u
+                code = codes[row, at]
+                second = codes[LIST_ROWS + row, at]
+                _, on_first, on_second = one_pair(code, second, everything, moments, columns)
+                results[0, at] = on_first
+                results[1, at] = on_second
+            return carry
+
+        lax.fori_loop(0, slots // UNROLL, step, 0)
+
+    def collect(side, slots):
+        def row(r):
+            return results[side, 0:slots, r, :]
+
+        for c in range(3):
+            sums_of[0:slots, c * SEG : (c + 1) * SEG] = row(c) + row(3 + c) + row(6 + c)
+        sums_of[0:slots, 3 * SEG : 4 * SEG] = row(9)
+        return split(sums_of[...], 3)
+
+    def near_collect(side):
+        sums_of[...] = jnp.zeros(sums_of.shape, F32)
+        return collect(side, NEAR_SLOTS)
+
+    def scatter(at, start, size, pieces):
+        hit = iota((size, SEG), 0) + start == jnp.broadcast_to(at, (size, SEG))
+        onehot = jnp.where(hit, 1.0, 0.0).astype(BF16)
+        return sum(dot(onehot, piece, NN) for piece in pieces)
+
+    def middle_of(c, start, size):
+        return everything[start : start + size, c, :]
+
+    sums_of[...] = jnp.zeros(sums_of.shape, F32)
+    run_list(FAR_ROW, FAR_SLOTS)
+    ghosts = groups * cap
+    second_at = codes_in[LIST_ROWS + FAR_ROW : LIST_ROWS + FAR_ROW + 1, :]
+    far_sums = scatter(second_at, blocks, ghosts, collect(1, FAR_SLOTS))
+    for c in range(3):
+        lanes = slice(c * SEG, (c + 1) * SEG)
+        force = middle_of(c, blocks, ghosts) * far_sums[:, 3 * SEG :] - far_sums[:, lanes]
+        for m in range(groups):
+            far_force[m, :, lanes] = force[m * cap : (m + 1) * cap, :] + far_extra[m, :, lanes]
 
     def node_of(b, end):
         return conn[end : end + 1, pl.ds(pl.multiple_of(b * SEG, SEG), SEG)]
@@ -476,8 +531,6 @@
             chosen[b, :, end * SEG : (end + 1) * SEG] = jnp.where(hit, 1.0, 0.0).astype(BF16)
         return carry
 
-    load.wait()
-    lax.fori_loop(0, blocks, choose, 0, unroll=2)
     await_greetings(me, rho, groups, cuts)
 
     def reaction_copy(m, other, at):
@@ -491,33 +544,46 @@
         )
 
     for_partners(me, rho, groups, cuts, lambda m, other: reaction_copy(m, other, slot).start())
-
-    def node_sums(first, last):
+    first_at = codes_in[FAR_ROW : FAR_ROW + 1, :] & 31
+    near_sums = scatter(first_at, 0, blocks, collect(0, FAR_SLOTS))
+    run_list(NEAR_ROW, NEAR_SLOTS)
+    first_at = codes_in[NEAR_ROW : NEAR_ROW + 1, :] & 31
+    near_sums = near_sums + scatter(first_at, 0, blocks, near_collect(0))
+    second_at = codes_in[LIST_ROWS + NEAR_ROW : LIST_ROWS + NEAR_ROW + 1, :]
+    near_sums = near_sums + scatter(second_at, 0, blocks, near_collect(1))
+    for c in range(3):
+        lanes = slice(c * SEG, (c + 1) * SEG)
+        force = middle_of(c, 0, blocks) * near_sums[:, 3 * SEG :] - near_sums[:, lanes]
+        near_force[:, lanes] = force + near_extra[:, lanes]
+    load.wait()
+    lax.fori_loop(0, blocks, choose, 0, unroll=2)
+
+    def node_step(g, eight, carry):
+        for i in range(8):
+            b = g * 8 + i
+            left = []
+            for end in range(2):
+                high = jnp.broadcast_to(node_of(b, end) >> 7, (blocks, SEG))
+                hit = iota((blocks, SEG), 0) == high
+                column = [
+                    jnp.where(hit, jnp.broadcast_to(piece[i : i + 1, :], (blocks, SEG)), 0.0)
+                    for piece in eight
+                ]
+                left.append(jnp.concatenate(column, axis=0).astype(BF16))
+            carry = carry + dot(jnp.concatenate(left, axis=1), chosen[b], NT)
+        return carry
+
+    def node_sums(fetch, parts):
         def step(g, carry):
-            at = pl.ds(pl.multiple_of(g * 8, 8), 8)
-            eight = [pieces[p, at, :] for p in range(first, last)]
-            for i in range(8):
-                b = g * 8 + i
-                left = []
-                for end in range(2):
-                    high = jnp.broadcast_to(node_of(b, end) >> 7, (blocks, SEG))
-                    hit = iota((blocks, SEG), 0) == high
-                    column = [
-                        jnp.where(hit, jnp.broadcast_to(piece[i : i + 1, :], (blocks, SEG)), 0.0)
-                        for piece in eight
-                    ]
-                    left.append(jnp.concatenate(column, axis=0).astype(BF16))
-                carry = carry + dot(jnp.concatenate(left, axis=1), chosen[b], NT)
-            return carry
-
-        start = jnp.zeros(((last - first) * blocks, SEG), F32)
-        sums = lax.fori_loop(0, blocks // 8, step, start)
-        rows = [sums[p * blocks : (p + 1) * blocks] for p in range(last - first)]
-        return [rows[p] + rows[p + 1] for p in range(0, last - first, 2)]
-
-    def set_piece(at, value):
-        for part, piece in enumerate(split(value, 2)):
-            pieces[at + part] = piece.astype(F32)
+            pieces = [piece.astype(F32) for value in fetch(g) for piece in split(value, 2)]
+            return node_step(g, pieces, carry)
+
+        sums = lax.fori_loop(0, blocks // 8, step, jnp.zeros((2 * parts * blocks, SEG), F32))
+        rows = [sums[p * blocks : (p + 1) * blocks] for p in range(2 * parts)]
+        return [rows[p] + rows[p + 1] for p in range(0, 2 * parts, 2)]
+
+    def eight_rows(g):
+        return pl.ds(pl.multiple_of(g * 8, 8), 8)
 
     value = [data[:, c * SEG : (c + 1) * SEG] for c in range(COMPS)]
     line = value[3:6]
@@ -527,8 +593,8 @@
     for c in range(3):
         u, v = (c + 1) % 3, (c + 2) % 3
         base[:, c * SEG : (c + 1) * SEG] = pull[u] * line[v] - pull[v] * line[u]
-    set_piece(6, jnp.sqrt(line[0] * line[0] + line[1] * line[1] + line[2] * line[2] + CORE_SQUARED))
-    drag = node_sums(6, 8)[0]
+    length[...] = jnp.sqrt(line[0] * line[0] + line[1] * line[1] + line[2] * line[2] + CORE_SQUARED)
+    drag = node_sums(lambda g: [length[eight_rows(g), :]], 1)[0]
     hit = iota(asked.shape, 1) == asked[...]
     onehot = jnp.transpose(jnp.where(hit, 1.0, 0.0))[:blocks, :].astype(BF16)
     for_partners(me, rho, groups, cuts, lambda m, other: reaction_copy(m, other, m).wait_recv())
@@ -539,32 +605,36 @@
         mine = mine + dot(onehot, piece, NN)
     shares[cut] = mine
 
-    def share_copy(d, at):
+    def share_copy(d, at, g):
         return pltpu.make_async_remote_copy(
-            src_ref=shares.at[cut],
-            dst_ref=shares.at[at],
-            send_sem=ssend.at[d - 1],
-            recv_sem=srecv.at[at],
+            src_ref=shares.at[cut, eight_rows(g)],
+            dst_ref=shares.at[at, eight_rows(g)],
+            send_sem=ssend.at[d - 1, g],
+            recv_sem=srecv.at[at, g],
             device_id=(me, lax.rem(cut + d, cuts)),
             device_id_type=MESH,
         )
 
-    for d in range(1, cuts):
-        share_copy(d, cut).start()
-    for d in range(1, cuts):
-        share_copy(d, lax.rem(cut - d + cuts, cuts)).wait_recv()
-    added = base[...]
-    for j in range(cuts):
-        added = added + shares[j]
-    for c in range(3):
-        set_piece(2 * c, added[:, c * SEG : (c + 1) * SEG])
-    sums = node_sums(0, 6)
+    for g in range(blocks // 8):
+        for d in range(1, cuts):
+            share_copy(d, cut, g).start()
+
+    def added(g):
+        for d in range(1, cuts):
+            share_copy(d, lax.rem(cut - d + cuts, cuts), g).wait_recv()
+        value = base[eight_rows(g), :]
+        for j in range(cuts):
+            value = value + shares[j, eight_rows(g), :]
+        return [value[:, c * SEG : (c + 1) * SEG] for c in range(3)]
+
+    sums = node_sums(added, 3)
     for c in range(3):
         speed = sums[c] / drag
         for b in range(blocks):
             velocity[c : c + 1, b * SEG : (b + 1) * SEG] = speed[b : b + 1, :]
-    for d in range(1, cuts):
-        share_copy(d, cut).wait_send()
+    for g in range(blocks // 8):
+        for d in range(1, cuts):
+            share_copy(d, cut, g).wait_send()
     for_partners(me, rho, groups, cuts, lambda m, other: reaction_copy(m, other, m).wait_send())
 
 
@@ -576,18 +646,19 @@
     width = COMPS * SEG
     shape = jax.ShapeDtypeStruct
     dma = pltpu.SemaphoreType.DMA
-    data, ghost, asked, codes, columns = pl.pallas_call(
+    data, ghost, asked, codes, extra, columns = pl.pallas_call(
         functools.partial(exchange_kernel, cuts, groups, cap, blocks),
         name="exchange",
         out_shape=(
             shape((blocks, width), F32),
             shape((groups, cap, SENT * SEG), F32),
             shape((groups * 8, SEG), I32),
-            shape((24, SEG), I32),
+            shape((2 * LIST_ROWS, SEG), I32),
+            shape((1, SEG), I32),
             shape((blocks, 6, SEG, SEG), F32),
         ),
         in_specs=[ANY] * 5,
-        out_specs=(VMEM,) * 5,
+        out_specs=(VMEM,) * 6,
         scratch_shapes=[
             pltpu.VMEM((3, nodes), F32),
             pltpu.VMEM((2, nodes), I32),
@@ -616,44 +687,45 @@
         stay(jnp.transpose(ghost_request[0])),
         stay(pair_list),
     )
-    near_force, far_force = run_pairs(codes, data, ghost, columns)
+    total_blocks = blocks + groups * cap
+    tables = [pltpu.VMEM((total_blocks, ROWS, SEG), F32)] * 2
+    list_scratch = [pltpu.SMEM((2 * LIST_ROWS, SEG), I32), dma]
+    near_extra, far_extra = pl.pallas_call(
+        extra_kernel,
+        name="extra",
+        out_shape=(shape((blocks, 3 * SEG), F32), shape((groups, cap, 3 * SEG), F32)),
+        in_specs=[SMEM, VMEM, VMEM, VMEM, VMEM],
+        out_specs=(VMEM,) * 2,
+        scratch_shapes=list_scratch + tables + [pltpu.VMEM((total_blocks, ROWS, SEG), F32)],
+        compiler_params=pltpu.CompilerParams(vmem_limit_bytes=PAIRS_VMEM),
+    )(extra, codes, data, ghost, columns)
     return pl.pallas_call(
         functools.partial(finish_kernel, cuts, groups, cap, blocks),
         name="finish",
         out_shape=shape((3, nodes), F32),
-        in_specs=[VMEM] * 4 + [ANY, SMEM],
+        in_specs=[VMEM] * 7 + [ANY, SMEM],
         out_specs=VMEM,
         scratch_shapes=[
             pltpu.VMEM((2, nodes), I32),
             dma,
+            *list_scratch,
+            *tables,
+            pltpu.VMEM((2, SEG, ROWS, SEG), F32),
+            pltpu.VMEM((SEG, 4 * SEG), F32),
+            pltpu.VMEM((blocks, 3 * SEG), F32),
+            pltpu.VMEM((groups, cap, 3 * SEG), F32),
             pltpu.VMEM((groups, cap, 3 * SEG), F32),
             pltpu.VMEM((groups * 8, 3 * SEG), F32),
             pltpu.VMEM((cuts, blocks, 3 * SEG), F32),
             pltpu.VMEM((blocks, SEG, 2 * SEG), BF16),
-            pltpu.VMEM((8, blocks, SEG), F32),
+            pltpu.VMEM((blocks, SEG), F32),
             pltpu.VMEM((blocks, 3 * SEG), F32),
-            dma((groups,)), dma((groups,)), dma((cuts,)), dma((cuts,)),
+            dma((groups,)), dma((groups,)), dma((cuts, blocks // 8)), dma((cuts, blocks // 8)),
         ],
         compiler_params=pltpu.CompilerParams(
             collective_id=1, has_side_effects=True, vmem_limit_bytes=FINISH_VMEM
         ),
-    )(near_force, far_force, asked, data, stay(connectivity), applied_stress)
-
-
-def run_pairs(codes, data, ghost, columns):
-    groups, cap, _ = ghost.shape
-    blocks = data.shape[0]
-    shape = jax.ShapeDtypeStruct
-    total_blocks = blocks + groups * cap
-    return pl.pallas_call(
-        pair_kernel,
-        name="pairs",
-        out_shape=(shape((blocks, 3 * SEG), F32), shape((groups, cap, 3 * SEG), F32)),
-        in_specs=[SMEM, VMEM, VMEM, VMEM],
-        out_specs=(VMEM,) * 2,
-        scratch_shapes=[pltpu.VMEM((total_blocks * ROWS, SEG), F32)] * 3,
-        compiler_params=pltpu.CompilerParams(vmem_limit_bytes=PAIRS_VMEM),
-    )(codes, data, ghost, columns)
+    )(near_extra, far_extra, codes, asked, data, ghost, columns, stay(connectivity), applied_stress)
 
 
 def solution(mesh):

time: 52 us -> 48.6 us (0.935)
  Pallas kernels: 51.2 us -> 47.8 us
    pallas_call x1, Pallas kernels: 9.41 us -> 0.56 us  [body(): pl.pallas_call(extra_kernel, name='extra', out_shape=(shape((blocks, 3 *...]
    pallas_call x1, Pallas kernels: 18.8 us -> 24.3 us  [body(): pl.pallas_call(functools.partial(finish_kernel, cuts, groups, cap, blocks...]
where the time goes in v4:
time: 48.6 us; the launch traced here: 48.5 us
  Pallas kernels  47.8 us (98%)
  local copies, waits for them, and re-layouts  0.64 us (1%)
    pallas_call x1, Pallas kernels, body(): pl.pallas_call(functools.partial(finish_kernel, cuts, groups, cap, blocks...  24.3 us
    pallas_call x1, Pallas kernels, body(): pl.pallas_call(functools.partial(exchange_kernel, cuts, groups, cap, bloc...  23 us

profile of v4, /device:TPU:1, one launch (start us, length us, event | category | flops | bytes accessed | tf_op | source)
XLA Modules:
  0.0 48.5 jit_solution(14037242611033146040)
XLA Ops:
  0.0 0.0 copy-start
  0.0 23.0 %exchange.1 = (f32[32,896]{1,0:T(8,128)S(1)}, f32[16,4,768]{2,1,0:T(4,128)S(1)}, s32[128,128]{1,0:T(8,128)S(1)}, s32[32,128]{1,0:T(8,128)S(1)}, s32[1,128]{1,0:T(1,128)S(1)}, /*index=5*/f32[32,6,128,128]{3,2,1,0:T(8,128)S(1)}) custom-call(f32[3,4096]{1,0:T(4,128)} %pos_in.1, s32[2,4096]{1,0:T(2,128)} %conn_in.3, s32[1,32]{1,0:T(1,128)} %bitcast.5, ...), custom_call_target="tpu_custom_call" | custom-call | tf_op jit(solution)/shard_map/exchange/pallas_call | solution.py:649
  23.0 0.6 %extra.1 = (f32[32,384]{1,0:T(8,128)S(1)}, f32[16,4,384]{2,1,0:T(4,128)S(1)}) custom-call(s32[1,128]{1,0:T(1,128)S(1)} %get-tuple-element.13.extra, s32[32,128]{1,0:T(8,128)S(1)} %get-tuple-element.14.codes_in, f32[32,896]{1,0:T(8,128)S(1)} %get-tuple-element.15.data, f32[16,4,768]{2,1,0:T(4,128)S(1)} %get-tuple-element.16.ghost, ...), custom_call_target="tpu_custom_call" | custom-call | tf_op jit(solution)/shard_map/extra/pallas_call | solution.py:693
  23.6 0.0 copy-done
  23.6 24.3 %finish.1 = f32[3,4096]{1,0:T(4,128)S(1)} custom-call(f32[32,384]{1,0:T(8,128)S(1)} %get-tuple-element.18.near_extra, f32[16,4,384]{2,1,0:T(4,128)S(1)} %get-tuple-element.19.far_extra, s32[32,128]{1,0:T(8,128)S(1)} %get-tuple-element.14.codes_in, s32[128,128]{1,0:T(8,128)S(1)} %get-tuple-element.20.asked, f32[32,896]{1,0:T(8,128)S(1)} %get-tuple-element.15.data, ...), custom_call_target="tpu_custom_call" | custom-call | tf_op jit(solution)/shard_map/finish/pallas_call | solution.py:702
  47.8 0.6 %copy.8 = f32[3,4096]{1,0:T(4,128)} copy(f32[3,4096]{1,0:T(4,128)S(1)} %finish.1) | data formatting | bytes 98304
Async XLA Ops:
  0.0 23.6 %copy-start = (f32[3,3]{1,0:T(4,128)S(1)}, f32[3,3]{1,0:T(4,128)}, u32[]{:S(2)}) copy-start(f32[3,3]{1,0:T(4,128)} %stress.1) | copy-start | bytes 112

commit v5 on v4

--- a/solution.py
+++ b/solution.py
@@ -12,7 +12,8 @@
 SENT = 6
 FIRST_ASK = 64
 ROWS = 16
-UNROLL = 8
+FAR_STEP = 40
+NEAR_STEP = 40
 FAR_SLOTS = 120
 NEAR_SLOTS = 40
 FAR_ROW = 8
@@ -476,10 +477,10 @@
     fill_tables(data, ghost, everything, moments)
     load_codes.wait()
 
-    def run_list(row, slots):
+    def run_list(row, slots, unroll):
         def step(i, carry):
-            for u in range(UNROLL):
-                at = i * UNROLL + u
+            for u in range(unroll):
+                at = i * unroll + u
                 code = codes[row, at]
                 second = codes[LIST_ROWS + row, at]
                 _, on_first, on_second = one_pair(code, second, everything, moments, columns)
@@ -487,7 +488,7 @@
                 results[1, at] = on_second
             return carry
 
-        lax.fori_loop(0, slots // UNROLL, step, 0)
+        lax.fori_loop(0, slots // unroll, step, 0)
 
     def collect(side, slots):
         def row(r):
@@ -511,7 +512,7 @@
         return everything[start : start + size, c, :]
 
     sums_of[...] = jnp.zeros(sums_of.shape, F32)
-    run_list(FAR_ROW, FAR_SLOTS)
+    run_list(FAR_ROW, FAR_SLOTS, FAR_STEP)
     ghosts = groups * cap
     second_at = codes_in[LIST_ROWS + FAR_ROW : LIST_ROWS + FAR_ROW + 1, :]
     far_sums = scatter(second_at, blocks, ghosts, collect(1, FAR_SLOTS))
@@ -546,7 +547,7 @@
     for_partners(me, rho, groups, cuts, lambda m, other: reaction_copy(m, other, slot).start())
     first_at = codes_in[FAR_ROW : FAR_ROW + 1, :] & 31
     near_sums = scatter(first_at, 0, blocks, collect(0, FAR_SLOTS))
-    run_list(NEAR_ROW, NEAR_SLOTS)
+    run_list(NEAR_ROW, NEAR_SLOTS, NEAR_STEP)
     first_at = codes_in[NEAR_ROW : NEAR_ROW + 1, :] & 31
     near_sums = near_sums + scatter(first_at, 0, blocks, near_collect(0))
     second_at = codes_in[LIST_ROWS + NEAR_ROW : LIST_ROWS + NEAR_ROW + 1, :]

time: 48.6 us -> 46.3 us (0.953)
  Pallas kernels: 47.8 us -> 45.5 us
    pallas_call x1, Pallas kernels: 24.3 us -> 22 us  [body(): pl.pallas_call(functools.partial(finish_kernel, cuts, groups, cap, blocks...]
where the time goes in v5:
time: 46.3 us; the launch traced here: 46.2 us
  Pallas kernels  45.5 us (98%)
  local copies, waits for them, and re-layouts  0.64 us (1%)
    pallas_call x1, Pallas kernels, body(): pl.pallas_call(functools.partial(exchange_kernel, cuts, groups, cap, bloc...  23 us
    pallas_call x1, Pallas kernels, body(): pl.pallas_call(functools.partial(finish_kernel, cuts, groups, cap, blocks...  22 us

profile of v5, /device:TPU:1, one launch (start us, length us, event | category | flops | bytes accessed | tf_op | source)
XLA Modules:
  0.0 46.2 jit_solution(12758909390432137062)
XLA Ops:
  0.0 0.0 copy-start
  0.0 23.0 %exchange.1 = (f32[32,896]{1,0:T(8,128)S(1)}, f32[16,4,768]{2,1,0:T(4,128)S(1)}, s32[128,128]{1,0:T(8,128)S(1)}, s32[32,128]{1,0:T(8,128)S(1)}, s32[1,128]{1,0:T(1,128)S(1)}, /*index=5*/f32[32,6,128,128]{3,2,1,0:T(8,128)S(1)}) custom-call(f32[3,4096]{1,0:T(4,128)} %pos_in.1, s32[2,4096]{1,0:T(2,128)} %conn_in.3, s32[1,32]{1,0:T(1,128)} %bitcast.5, ...), custom_call_target="tpu_custom_call" | custom-call | tf_op jit(solution)/shard_map/exchange/pallas_call | solution.py:650
  23.0 0.6 %extra.1 = (f32[32,384]{1,0:T(8,128)S(1)}, f32[16,4,384]{2,1,0:T(4,128)S(1)}) custom-call(s32[1,128]{1,0:T(1,128)S(1)} %get-tuple-element.13.extra, s32[32,128]{1,0:T(8,128)S(1)} %get-tuple-element.14.codes_in, f32[32,896]{1,0:T(8,128)S(1)} %get-tuple-element.15.data, f32[16,4,768]{2,1,0:T(4,128)S(1)} %get-tuple-element.16.ghost, ...), custom_call_target="tpu_custom_call" | custom-call | tf_op jit(solution)/shard_map/extra/pallas_call | solution.py:694
  23.6 0.0 copy-done
  23.6 22.0 %finish.1 = f32[3,4096]{1,0:T(4,128)S(1)} custom-call(f32[32,384]{1,0:T(8,128)S(1)} %get-tuple-element.18.near_extra, f32[16,4,384]{2,1,0:T(4,128)S(1)} %get-tuple-element.19.far_extra, s32[32,128]{1,0:T(8,128)S(1)} %get-tuple-element.14.codes_in, s32[128,128]{1,0:T(8,128)S(1)} %get-tuple-element.20.asked, f32[32,896]{1,0:T(8,128)S(1)} %get-tuple-element.15.data, ...), custom_call_target="tpu_custom_call" | custom-call | tf_op jit(solution)/shard_map/finish/pallas_call | solution.py:703
  45.5 0.6 %copy.8 = f32[3,4096]{1,0:T(4,128)} copy(f32[3,4096]{1,0:T(4,128)S(1)} %finish.1) | data formatting | bytes 98304
Async XLA Ops:
  0.0 23.6 %copy-start = (f32[3,3]{1,0:T(4,128)S(1)}, f32[3,3]{1,0:T(4,128)}, u32[]{:S(2)}) copy-start(f32[3,3]{1,0:T(4,128)} %stress.1) | copy-start | bytes 112

commit v6 on v5

--- a/solution.py
+++ b/solution.py
@@ -12,7 +12,9 @@
 SENT = 6
 FIRST_ASK = 64
 ROWS = 16
-FAR_STEP = 40
+FIRST_SLOTS = 72
+FIRST_STEP = 36
+LAST_STEP = 48
 NEAR_STEP = 40
 FAR_SLOTS = 120
 NEAR_SLOTS = 40
@@ -135,36 +137,94 @@
 
 
 def spread_columns(flat, columns):
-    blocks = columns.shape[0]
-
     def step(block, carry):
-        tall = jnp.transpose(flat[pl.ds(pl.multiple_of(block * 8, 8), 8), :])
+        rows = flat[pl.ds(pl.multiple_of(block * 8, 8), 8), :]
         for c in range(6):
-            columns[block, c] = jnp.broadcast_to(tall[:, c : c + 1], (SEG, SEG))
+            columns[block, c] = jnp.transpose(jnp.broadcast_to(rows[c : c + 1, :], (SEG, SEG)))
         return carry
 
-    lax.fori_loop(0, blocks, step, 0, unroll=2)
-
-
-def for_partners(me, rho, groups, cuts, run):
+    lax.fori_loop(0, columns.shape[0], step, 0, unroll=8)
+
+
+def node_of(conn, b, end):
+    return conn[end : end + 1, pl.ds(pl.multiple_of(b * SEG, SEG), SEG)]
+
+
+def eight_rows(g):
+    return pl.ds(pl.multiple_of(g * 8, 8), 8)
+
+
+def choose_nodes(conn, chosen):
+    def choose(b, carry):
+        for end in range(2):
+            low = jnp.broadcast_to(node_of(conn, b, end) & (SEG - 1), (SEG, SEG))
+            hit = iota((SEG, SEG), 0) == low
+            chosen[b, :, end * SEG : (end + 1) * SEG] = jnp.where(hit, 1.0, 0.0).astype(BF16)
+        return carry
+
+    lax.fori_loop(0, chosen.shape[0], choose, 0, unroll=2)
+
+
+def node_sums(conn, chosen, fetch, parts):
+    blocks = chosen.shape[0]
+
+    def step(g, carry):
+        pieces = [piece.astype(F32) for value in fetch(g) for piece in split(value, 2)]
+        for i in range(8):
+            b = g * 8 + i
+            left = []
+            for end in range(2):
+                high = jnp.broadcast_to(node_of(conn, b, end) >> 7, (blocks, SEG))
+                hit = iota((blocks, SEG), 0) == high
+                column = [
+                    jnp.where(hit, jnp.broadcast_to(piece[i : i + 1, :], (blocks, SEG)), 0.0)
+                    for piece in pieces
+                ]
+                left.append(jnp.concatenate(column, axis=0).astype(BF16))
+            carry = carry + dot(jnp.concatenate(left, axis=1), chosen[b], NT)
+        return carry
+
+    sums = lax.fori_loop(0, blocks // 8, step, jnp.zeros((2 * parts * blocks, SEG), F32))
+    rows = [sums[p * blocks : (p + 1) * blocks] for p in range(2 * parts)]
+    return [rows[p] + rows[p + 1] for p in range(0, 2 * parts, 2)]
+
+
+def outer_force(values, stress):
+    line = values[3:6]
+    burgers = burgers_of(values[6])
+    sigma = [[0.5 * (stress[a, b] + stress[b, a]) for b in range(3)] for a in range(3)]
+    pull = [sigma[a][0] * burgers[0] + sigma[a][1] * burgers[1] + sigma[a][2] * burgers[2] for a in range(3)]
+    forces = []
+    for c in range(3):
+        u, v = (c + 1) % 3, (c + 2) % 3
+        forces.append(pull[u] * line[v] - pull[v] * line[u])
+    return forces
+
+
+def partner(i, me, rho, groups, cuts):
+    half = groups // 2
+    hop = jnp.where(lax.rem(i, 2) == 0, half + lax.div(i, 2), half - lax.div(i + 1, 2))
+    m = lax.rem(lax.div(me, cuts) + hop, groups)
+    return m, m * cuts + rho
+
+
+def for_partners(me, rho, groups, cuts, run, first=0, last=None):
     def step(i, carry):
-        hop = jnp.where(lax.rem(i, 2) == 0, groups // 2 + lax.div(i, 2), groups // 2 - lax.div(i + 1, 2))
-        m = lax.rem(lax.div(me, cuts) + hop, groups)
-        other = m * cuts + rho
+        m, other = partner(i, me, rho, groups, cuts)
 
         @pl.when(other != me)
         def _():
-            run(m, other)
+            run(i, m, other)
 
         return carry
 
-    lax.fori_loop(0, groups, step, 0)
+    lax.fori_loop(first, groups if last is None else last, step, 0)
 
 
 def greet(me, cut, rho, groups, cuts):
     barrier = pltpu.get_barrier_semaphore()
 
-    def signal(m, other):
+    def signal(i, m, other):
         pl.semaphore_signal(barrier, inc=1, device_id=(other, cut), device_id_type=MESH)
 
     for_partners(me, rho, groups, cuts, signal)
@@ -199,6 +259,7 @@
 
 
 def share_pairs(first, second, own_row, kinds, me, cut, cuts, cap, blocks):
+    slot_of_me = me // cuts
     used = first >= 0
     ghost = second >= blocks
     slot = jnp.maximum(second - blocks, 0)
@@ -225,8 +286,13 @@
     part_size = (count(near) + cuts - 1) >> 2
     rank = prefix(near) - cut * part_size
     mine_near = near & (rank >= 0) & (rank < part_size)
-    far_spot = prefix(mine_far)
-    fits = (mine_far & (far_spot < FAR_SLOTS)) | (mine_near & (rank < NEAR_SLOTS))
+    hop = ((owner >> 2) - slot_of_me) & 15
+    distant = (hop >= 4) & (hop < 12)
+    mine_first = mine_far & distant
+    mine_last = mine_far & jnp.logical_not(distant)
+    far_spot = jnp.where(distant, prefix(mine_first), count(mine_first) + prefix(mine_last))
+    room = jnp.where(distant, FIRST_SLOTS, FAR_SLOTS)
+    fits = (mine_far & (far_spot < room)) | (mine_near & (rank < NEAR_SLOTS))
     mine = mine_far | mine_near
     rest = mine & jnp.logical_not(fits)
     lanes = first.shape[1]
@@ -254,21 +320,21 @@
 def exchange_kernel(
     cuts, groups, cap, blocks,
     pos_in, conn_in, burg_in, req_in, pairs_in,
-    data, ghost, asked, codes, extra, columns,
-    pos, conn, burg, req, pairs, links, flat, wide, rows, heard, table, plist, stage, ordered,
+    data, ghost, asked, codes, extra, columns, chosen, drag, conn,
+    pos, burg, req, pairs, links, flat, length, wide, rows, heard, table, plist, stage, ordered,
     isem, rsend, rrecv, psend, precv, bsend, brecv,
 ):
     me = lax.axis_index("cell")
     cut = lax.axis_index("cuts")
     rho = lax.rem(cut - lax.rem(me, cuts) + cuts, cuts)
     slot = lax.div(me, cuts)
+    heard[slot] = jnp.full(heard.shape[1:], -1, I32)
+    ghost[slot] = jnp.zeros(ghost.shape[1:], F32)
+    greet(me, cut, rho, groups, cuts)
     inputs = [(req_in, req), (burg_in, burg), (pairs_in, pairs), (conn_in, conn), (pos_in, pos)]
     loads = [pltpu.make_async_copy(src, dst, isem.at[i]) for i, (src, dst) in enumerate(inputs)]
     for load in loads:
         load.start()
-    heard[...] = jnp.full(heard.shape, -1, I32)
-    ghost[...] = jnp.zeros(ghost.shape, F32)
-    greet(me, cut, rho, groups, cuts)
     for load in loads[:3]:
         load.wait()
     fill_requests(req, burg, wide, rows)
@@ -298,7 +364,7 @@
             device_id_type=MESH,
         )
 
-    for_partners(me, rho, groups, cuts, lambda m, other: request_copy(m, other, slot).start())
+    for_partners(me, rho, groups, cuts, lambda i, m, other: request_copy(m, other, slot).start())
     for d in range(1, cuts):
         pair_copy(d, cut).start()
     for load in loads[3:]:
@@ -313,33 +379,44 @@
         flat[pl.ds(c, blocks, stride=8), :] = values[c]
         for part, piece in enumerate(split(values[c], 3)):
             table[part * blocks : (part + 1) * blocks, lanes] = piece
-    for_partners(me, rho, groups, cuts, lambda m, other: request_copy(m, other, m).wait_recv())
+    def block_copy(i, m, other, at):
+        return pltpu.make_async_remote_copy(
+            src_ref=stage.at[i],
+            dst_ref=ghost.at[at],
+            send_sem=bsend.at[i],
+            recv_sem=brecv.at[at],
+            device_id=(other, cut),
+            device_id_type=MESH,
+        )
+
+    def serve(first, last):
+        def arrived(i, m, other):
+            request_copy(m, other, m).wait_recv()
+
+        for_partners(me, rho, groups, cuts, arrived, first, last)
+        count = last - first
+        order = [partner(i, me, rho, groups, cuts)[0] for i in range(first, last)]
+        asks = jnp.concatenate([heard[m] for m in order], axis=0)
+        columns_of = [asks[:, FIRST_ASK + t : FIRST_ASK + t + 1] for t in range(cap)]
+        wanted = jnp.concatenate([jnp.broadcast_to(column, (count, SEG)) for column in columns_of], axis=0)
+        lane = iota(wanted.shape, 1)
+        hit = ((lane & (blocks - 1)) == wanted) & (lane < 3 * blocks)
+        onehot = jnp.where(hit, 1.0, 0.0).astype(BF16)
+        for c in range(SENT):
+            lanes = slice(c * SEG, (c + 1) * SEG)
+            got = dot(onehot, table[:, lanes], NN)
+            for t in range(cap):
+                stage[first:last, t, lanes] = got[t * count : (t + 1) * count, :]
+        for_partners(me, rho, groups, cuts, lambda i, m, other: block_copy(i, m, other, slot).start(), first, last)
+
+    serve(groups // 2, groups)
+    serve(0, groups // 2)
     hear = jnp.concatenate([heard[m] for m in range(groups)], axis=0)
     asked[...] = jnp.full(asked.shape, -1, I32)
     for t in range(cap):
         column = hear[:, FIRST_ASK + t : FIRST_ASK + t + 1]
         asked[pl.ds(t, groups, stride=8), :] = jnp.broadcast_to(column, (groups, SEG))
 
-    lane = iota(asked.shape, 1)
-    hit = ((lane & (blocks - 1)) == asked[...]) & (lane < 3 * blocks)
-    onehot = jnp.where(hit, 1.0, 0.0).astype(BF16)
-    for c in range(SENT):
-        lanes = slice(c * SEG, (c + 1) * SEG)
-        got = dot(onehot, table[:, lanes], NN)
-        for m in range(groups):
-            stage[m, :, lanes] = got[m * 8 : m * 8 + cap, :]
-
-    def block_copy(m, other, at):
-        return pltpu.make_async_remote_copy(
-            src_ref=stage.at[m],
-            dst_ref=ghost.at[at],
-            send_sem=bsend.at[m],
-            recv_sem=brecv.at[at],
-            device_id=(other, cut),
-            device_id_type=MESH,
-        )
-
-    for_partners(me, rho, groups, cuts, lambda m, other: block_copy(m, other, slot).start())
     spread_columns(flat, columns)
     for d in range(1, cuts):
         pair_copy(d, lax.rem(cut - d + cuts, cuts)).wait_recv()
@@ -352,9 +429,13 @@
     listed, total = share_pairs(ordered[0], ordered[1], own_row, kinds, me, cut, cuts, cap, blocks)
     codes[...] = listed
     extra[...] = jnp.broadcast_to(total, extra.shape)
-    for_partners(me, rho, groups, cuts, lambda m, other: block_copy(m, other, m).wait_recv())
-    for_partners(me, rho, groups, cuts, lambda m, other: block_copy(m, other, m).wait_send())
-    for_partners(me, rho, groups, cuts, lambda m, other: request_copy(m, other, m).wait_send())
+    choose_nodes(conn, chosen)
+    line = [data[:, c * SEG : (c + 1) * SEG] for c in range(3, 6)]
+    length[...] = jnp.sqrt(line[0] * line[0] + line[1] * line[1] + line[2] * line[2] + CORE_SQUARED)
+    drag[...] = node_sums(conn, chosen, lambda g: [length[eight_rows(g), :]], 1)[0]
+    for_partners(me, rho, groups, cuts, lambda i, m, other: block_copy(i, m, other, m).wait_recv())
+    for_partners(me, rho, groups, cuts, lambda i, m, other: block_copy(i, m, other, m).wait_send())
+    for_partners(me, rho, groups, cuts, lambda i, m, other: request_copy(m, other, m).wait_send())
     for d in range(1, cuts):
         pair_copy(d, cut).wait_send()
 
@@ -424,7 +505,9 @@
     near_force[...] = jnp.zeros(near_force.shape, F32)
     far_force[...] = jnp.zeros(far_force.shape, F32)
 
-    @pl.when(extra[0, 0] > 0)
+    left = jnp.max(extra[...].astype(F32)).astype(I32)
+
+    @pl.when(left > 0)
     def _():
         load = pltpu.make_async_copy(codes_in, codes, sem)
         load.start()
@@ -440,7 +523,7 @@
             total[second] = total[second] + on_second
             return carry
 
-        lax.fori_loop(0, extra[0, 0], body, 0)
+        lax.fori_loop(0, left, body, 0)
 
         def take(ref, row, start, rows):
             return ref[start : start + rows, row, :]
@@ -459,28 +542,26 @@
 
 def finish_kernel(
     cuts, groups, cap, blocks,
-    near_extra, far_extra, codes_in, asked, data, ghost, columns, conn_in, stress,
+    near_extra, far_extra, codes_in, asked, data, ghost, columns, conn, chosen, drag, stress,
     velocity,
-    conn, isem, codes, csem, everything, moments, results, sums_of, near_force, far_force, back, table, shares, chosen, length, base, bsend, brecv, ssend, srecv,
+    base, codes, csem, everything, moments, results, sums_of, near_force, first_force, last_force, back, table, shares, bsend, brecv, ssend, srecv,
 ):
     me = lax.axis_index("cell")
     cut = lax.axis_index("cuts")
     rho = lax.rem(cut - lax.rem(me, cuts) + cuts, cuts)
     slot = lax.div(me, cuts)
-    load = pltpu.make_async_copy(conn_in, conn, isem)
-    load.start()
     load_codes = pltpu.make_async_copy(codes_in, codes, csem)
     load_codes.start()
-    back[...] = jnp.zeros(back.shape, F32)
+    back[slot] = jnp.zeros(back.shape[1:], F32)
     greet(me, cut, rho, groups, cuts)
     table[...] = jnp.zeros(table.shape, F32)
     fill_tables(data, ghost, everything, moments)
     load_codes.wait()
 
-    def run_list(row, slots, unroll):
+    def run_list(row, begin, slots, unroll):
         def step(i, carry):
             for u in range(unroll):
-                at = i * unroll + u
+                at = begin + i * unroll + u
                 code = codes[row, at]
                 second = codes[LIST_ROWS + row, at]
                 _, on_first, on_second = one_pair(code, second, everything, moments, columns)
@@ -490,18 +571,16 @@
 
         lax.fori_loop(0, slots // unroll, step, 0)
 
-    def collect(side, slots):
+    def collect(side, begin, slots):
         def row(r):
-            return results[side, 0:slots, r, :]
-
+            return results[side, begin : begin + slots, r, :]
+
+        at = slice(begin, begin + slots)
+        sums_of[...] = jnp.zeros(sums_of.shape, F32)
         for c in range(3):
-            sums_of[0:slots, c * SEG : (c + 1) * SEG] = row(c) + row(3 + c) + row(6 + c)
-        sums_of[0:slots, 3 * SEG : 4 * SEG] = row(9)
+            sums_of[at, c * SEG : (c + 1) * SEG] = row(c) + row(3 + c) + row(6 + c)
+        sums_of[at, 3 * SEG : 4 * SEG] = row(9)
         return split(sums_of[...], 3)
-
-    def near_collect(side):
-        sums_of[...] = jnp.zeros(sums_of.shape, F32)
-        return collect(side, NEAR_SLOTS)
 
     def scatter(at, start, size, pieces):
         hit = iota((size, SEG), 0) + start == jnp.broadcast_to(at, (size, SEG))
@@ -511,32 +590,19 @@
     def middle_of(c, start, size):
         return everything[start : start + size, c, :]
 
-    sums_of[...] = jnp.zeros(sums_of.shape, F32)
-    run_list(FAR_ROW, FAR_SLOTS, FAR_STEP)
     ghosts = groups * cap
     second_at = codes_in[LIST_ROWS + FAR_ROW : LIST_ROWS + FAR_ROW + 1, :]
-    far_sums = scatter(second_at, blocks, ghosts, collect(1, FAR_SLOTS))
-    for c in range(3):
-        lanes = slice(c * SEG, (c + 1) * SEG)
-        force = middle_of(c, blocks, ghosts) * far_sums[:, 3 * SEG :] - far_sums[:, lanes]
-        for m in range(groups):
-            far_force[m, :, lanes] = force[m * cap : (m + 1) * cap, :] + far_extra[m, :, lanes]
-
-    def node_of(b, end):
-        return conn[end : end + 1, pl.ds(pl.multiple_of(b * SEG, SEG), SEG)]
-
-    def choose(b, carry):
-        for end in range(2):
-            low = jnp.broadcast_to(node_of(b, end) & (SEG - 1), (SEG, SEG))
-            hit = iota((SEG, SEG), 0) == low
-            chosen[b, :, end * SEG : (end + 1) * SEG] = jnp.where(hit, 1.0, 0.0).astype(BF16)
-        return carry
-
-    await_greetings(me, rho, groups, cuts)
-
-    def reaction_copy(m, other, at):
+
+    def far_result(sums, out):
+        for c in range(3):
+            lanes = slice(c * SEG, (c + 1) * SEG)
+            force = middle_of(c, blocks, ghosts) * sums[:, 3 * SEG :] - sums[:, lanes]
+            for m in range(groups):
+                out[m, :, lanes] = force[m * cap : (m + 1) * cap, :] + far_extra[m, :, lanes]
+
+    def reaction_copy(source, m, other, at):
         return pltpu.make_async_remote_copy(
-            src_ref=far_force.at[m],
+            src_ref=source.at[m],
             dst_ref=back.at[at],
             send_sem=bsend.at[m],
             recv_sem=brecv.at[at],
@@ -544,61 +610,40 @@
             device_id_type=MESH,
         )
 
-    for_partners(me, rho, groups, cuts, lambda m, other: reaction_copy(m, other, slot).start())
+    def send_first(i, m, other):
+        reaction_copy(first_force, m, other, slot).start()
+
+    def send_last(i, m, other):
+        reaction_copy(last_force, m, other, slot).start()
+
+    half = groups // 2
+    run_list(FAR_ROW, 0, FIRST_SLOTS, FIRST_STEP)
+    far_sums = scatter(second_at, blocks, ghosts, collect(1, 0, FIRST_SLOTS))
+    far_result(far_sums, first_force)
+    await_greetings(me, rho, groups, cuts)
+    for_partners(me, rho, groups, cuts, send_first, 0, half)
+    run_list(FAR_ROW, FIRST_SLOTS, FAR_SLOTS - FIRST_SLOTS, LAST_STEP)
+    late = collect(1, FIRST_SLOTS, FAR_SLOTS - FIRST_SLOTS)
+    far_result(far_sums + scatter(second_at, blocks, ghosts, late), last_force)
+    for_partners(me, rho, groups, cuts, send_last, half, groups)
     first_at = codes_in[FAR_ROW : FAR_ROW + 1, :] & 31
-    near_sums = scatter(first_at, 0, blocks, collect(0, FAR_SLOTS))
-    run_list(NEAR_ROW, NEAR_SLOTS, NEAR_STEP)
+    near_sums = scatter(first_at, 0, blocks, collect(0, 0, FAR_SLOTS))
+    run_list(NEAR_ROW, 0, NEAR_SLOTS, NEAR_STEP)
     first_at = codes_in[NEAR_ROW : NEAR_ROW + 1, :] & 31
-    near_sums = near_sums + scatter(first_at, 0, blocks, near_collect(0))
+    near_sums = near_sums + scatter(first_at, 0, blocks, collect(0, 0, NEAR_SLOTS))
     second_at = codes_in[LIST_ROWS + NEAR_ROW : LIST_ROWS + NEAR_ROW + 1, :]
-    near_sums = near_sums + scatter(second_at, 0, blocks, near_collect(1))
+    near_sums = near_sums + scatter(second_at, 0, blocks, collect(1, 0, NEAR_SLOTS))
     for c in range(3):
         lanes = slice(c * SEG, (c + 1) * SEG)
         force = middle_of(c, 0, blocks) * near_sums[:, 3 * SEG :] - near_sums[:, lanes]
         near_force[:, lanes] = force + near_extra[:, lanes]
-    load.wait()
-    lax.fori_loop(0, blocks, choose, 0, unroll=2)
-
-    def node_step(g, eight, carry):
-        for i in range(8):
-            b = g * 8 + i
-            left = []
-            for end in range(2):
-                high = jnp.broadcast_to(node_of(b, end) >> 7, (blocks, SEG))
-                hit = iota((blocks, SEG), 0) == high
-                column = [
-                    jnp.where(hit, jnp.broadcast_to(piece[i : i + 1, :], (blocks, SEG)), 0.0)
-                    for piece in eight
-                ]
-                left.append(jnp.concatenate(column, axis=0).astype(BF16))
-            carry = carry + dot(jnp.concatenate(left, axis=1), chosen[b], NT)
-        return carry
-
-    def node_sums(fetch, parts):
-        def step(g, carry):
-            pieces = [piece.astype(F32) for value in fetch(g) for piece in split(value, 2)]
-            return node_step(g, pieces, carry)
-
-        sums = lax.fori_loop(0, blocks // 8, step, jnp.zeros((2 * parts * blocks, SEG), F32))
-        rows = [sums[p * blocks : (p + 1) * blocks] for p in range(2 * parts)]
-        return [rows[p] + rows[p + 1] for p in range(0, 2 * parts, 2)]
-
-    def eight_rows(g):
-        return pl.ds(pl.multiple_of(g * 8, 8), 8)
-
-    value = [data[:, c * SEG : (c + 1) * SEG] for c in range(COMPS)]
-    line = value[3:6]
-    burgers = burgers_of(value[6])
-    sigma = [[0.5 * (stress[a, b] + stress[b, a]) for b in range(3)] for a in range(3)]
-    pull = [sigma[a][0] * burgers[0] + sigma[a][1] * burgers[1] + sigma[a][2] * burgers[2] for a in range(3)]
-    for c in range(3):
-        u, v = (c + 1) % 3, (c + 2) % 3
-        base[:, c * SEG : (c + 1) * SEG] = pull[u] * line[v] - pull[v] * line[u]
-    length[...] = jnp.sqrt(line[0] * line[0] + line[1] * line[1] + line[2] * line[2] + CORE_SQUARED)
-    drag = node_sums(lambda g: [length[eight_rows(g), :]], 1)[0]
+
+    values = [data[:, c * SEG : (c + 1) * SEG] for c in range(COMPS)]
+    for c, force in enumerate(outer_force(values, stress)):
+        base[:, c * SEG : (c + 1) * SEG] = force
     hit = iota(asked.shape, 1) == asked[...]
     onehot = jnp.transpose(jnp.where(hit, 1.0, 0.0))[:blocks, :].astype(BF16)
-    for_partners(me, rho, groups, cuts, lambda m, other: reaction_copy(m, other, m).wait_recv())
+    for_partners(me, rho, groups, cuts, lambda i, m, other: reaction_copy(last_force, m, other, m).wait_recv())
     for m in range(groups):
         table[m * 8 : m * 8 + cap, :] = back[m]
     mine = near_force[...]
@@ -628,15 +673,16 @@
             value = value + shares[j, eight_rows(g), :]
         return [value[:, c * SEG : (c + 1) * SEG] for c in range(3)]
 
-    sums = node_sums(added, 3)
+    sums = node_sums(conn, chosen, added, 3)
+    slow = drag[...]
     for c in range(3):
-        speed = sums[c] / drag
+        speed = sums[c] / slow
         for b in range(blocks):
             velocity[c : c + 1, b * SEG : (b + 1) * SEG] = speed[b : b + 1, :]
     for g in range(blocks // 8):
         for d in range(1, cuts):
             share_copy(d, cut, g).wait_send()
-    for_partners(me, rho, groups, cuts, lambda m, other: reaction_copy(m, other, m).wait_send())
+    for_partners(me, rho, groups, cuts, lambda i, m, other: reaction_copy(last_force, m, other, m).wait_send())
 
 
 def body(cuts, node_positions, connectivity, burgers_index, applied_stress, ghost_request, pair_list):
@@ -647,7 +693,7 @@
     width = COMPS * SEG
     shape = jax.ShapeDtypeStruct
     dma = pltpu.SemaphoreType.DMA
-    data, ghost, asked, codes, extra, columns = pl.pallas_call(
+    data, ghost, asked, codes, extra, columns, chosen, drag, conn = pl.pallas_call(
         functools.partial(exchange_kernel, cuts, groups, cap, blocks),
         name="exchange",
         out_shape=(
@@ -657,17 +703,20 @@
             shape((2 * LIST_ROWS, SEG), I32),
             shape((1, SEG), I32),
             shape((blocks, 6, SEG, SEG), F32),
+            shape((blocks, SEG, 2 * SEG), BF16),
+            shape((blocks, SEG), F32),
+            shape(connectivity.shape, I32),
         ),
         in_specs=[ANY] * 5,
-        out_specs=(VMEM,) * 6,
+        out_specs=(VMEM,) * 9,
         scratch_shapes=[
             pltpu.VMEM((3, nodes), F32),
-            pltpu.VMEM((2, nodes), I32),
             pltpu.VMEM((1, blocks), I32),
             pltpu.VMEM((cap, owners), I32),
             pltpu.VMEM(pair_list.shape, I32),
             pltpu.VMEM((2, blocks, SEG), I32),
             pltpu.VMEM((blocks * 8, SEG), F32),
+            pltpu.VMEM((blocks, SEG), F32),
             pltpu.VMEM((1, SEG), I32),
             pltpu.VMEM((owners, 1, SEG), I32),
             pltpu.VMEM((groups, 1, SEG), I32),
@@ -695,7 +744,7 @@
         extra_kernel,
         name="extra",
         out_shape=(shape((blocks, 3 * SEG), F32), shape((groups, cap, 3 * SEG), F32)),
-        in_specs=[SMEM, VMEM, VMEM, VMEM, VMEM],
+        in_specs=[VMEM, VMEM, VMEM, VMEM, VMEM],
         out_specs=(VMEM,) * 2,
         scratch_shapes=list_scratch + tables + [pltpu.VMEM((total_blocks, ROWS, SEG), F32)],
         compiler_params=pltpu.CompilerParams(vmem_limit_bytes=PAIRS_VMEM),
@@ -704,11 +753,10 @@
         functools.partial(finish_kernel, cuts, groups, cap, blocks),
         name="finish",
         out_shape=shape((3, nodes), F32),
-        in_specs=[VMEM] * 7 + [ANY, SMEM],
+        in_specs=[VMEM] * 10 + [SMEM],
         out_specs=VMEM,
         scratch_shapes=[
-            pltpu.VMEM((2, nodes), I32),
-            dma,
+            pltpu.VMEM((blocks, 3 * SEG), F32),
             *list_scratch,
             *tables,
             pltpu.VMEM((2, SEG, ROWS, SEG), F32),
@@ -716,17 +764,15 @@
             pltpu.VMEM((blocks, 3 * SEG), F32),
             pltpu.VMEM((groups, cap, 3 * SEG), F32),
             pltpu.VMEM((groups, cap, 3 * SEG), F32),
+            pltpu.VMEM((groups, cap, 3 * SEG), F32),
             pltpu.VMEM((groups * 8, 3 * SEG), F32),
             pltpu.VMEM((cuts, blocks, 3 * SEG), F32),
-            pltpu.VMEM((blocks, SEG, 2 * SEG), BF16),
-            pltpu.VMEM((blocks, SEG), F32),
-            pltpu.VMEM((blocks, 3 * SEG), F32),
             dma((groups,)), dma((groups,)), dma((cuts, blocks // 8)), dma((cuts, blocks // 8)),
         ],
         compiler_params=pltpu.CompilerParams(
             collective_id=1, has_side_effects=True, vmem_limit_bytes=FINISH_VMEM
         ),
-    )(near_extra, far_extra, codes, asked, data, ghost, columns, stay(connectivity), applied_stress)
+    )(near_extra, far_extra, codes, asked, data, ghost, columns, conn, chosen, drag, applied_stress)
 
 
 def solution(mesh):

time: 46.3 us -> 44.4 us (0.959)
  Pallas kernels: 45.5 us -> 43.7 us
    pallas_call x1, Pallas kernels: 22 us -> 21.3 us  [body(): pl.pallas_call(functools.partial(finish_kernel, cuts, groups, cap, blocks...]
    pallas_call x1, Pallas kernels: 23 us -> 22.3 us  [body(): pl.pallas_call(functools.partial(exchange_kernel, cuts, groups, cap, bloc...]
where the time goes in v6:
time: 44.4 us; the launch traced here: 44.3 us
  Pallas kernels  43.7 us (98%)
  local copies, waits for them, and re-layouts  0.64 us (1%)
    pallas_call x1, Pallas kernels, body(): pl.pallas_call(functools.partial(exchange_kernel, cuts, groups, cap, bloc...  22.3 us
    pallas_call x1, Pallas kernels, body(): pl.pallas_call(functools.partial(finish_kernel, cuts, groups, cap, blocks...  21.3 us

profile of v6, /device:TPU:1, one launch (start us, length us, event | category | flops | bytes accessed | tf_op | source)
XLA Modules:
  0.0 44.3 jit_solution(11476311788296920555)
XLA Ops:
  0.0 0.0 copy-start
  0.0 22.3 %exchange.1 = (f32[32,896]{1,0:T(8,128)S(1)}, f32[16,4,768]{2,1,0:T(4,128)S(1)}, s32[128,128]{1,0:T(8,128)S(1)}, s32[32,128]{1,0:T(8,128)S(1)}, s32[1,128]{1,0:T...) custom-call(f32[3,4096]{1,0:T(4,128)} %pos_in.1, ...), custom_call_target="tpu_custom_call" | custom-call | tf_op jit(solution)/shard_map/exchange/pallas_call | solution.py:696
  22.3 0.1 extra.1
  22.4 0.0 copy-done
  22.4 21.3 %finish.1 = f32[3,4096]{1,0:T(4,128)S(1)} custom-call(f32[32,384]{1,0:T(8,128)S(1)} %get-tuple-element.21.near_extra, f32[16,4,384]{2,1,0:T(4,128)S(1)} %get-tuple-element.22.far_extra, s32[32,128]{1,0:T(8,128)S(1)} %get-tuple-element.17.codes_in, s32[128,128]{1,0:T(8,128)S(1)} %get-tuple-element.23.asked, f32[32,896]{1,0:T(8,128)S(1)} %get-tuple-element.18.data, ...), custom_call_target="tpu_custom_call" | custom-call | tf_op jit(solution)/shard_map/finish/pallas_call | solution.py:752
  43.7 0.6 %copy.8 = f32[3,4096]{1,0:T(4,128)} copy(f32[3,4096]{1,0:T(4,128)S(1)} %finish.1) | data formatting | bytes 98304
Async XLA Ops:
  0.0 22.4 %copy-start = (f32[3,3]{1,0:T(4,128)S(1)}, f32[3,3]{1,0:T(4,128)}, u32[]{:S(2)}) copy-start(f32[3,3]{1,0:T(4,128)} %stress.1) | copy-start | bytes 112

commit v7 on v6

--- a/solution.py
+++ b/solution.py
@@ -14,9 +14,9 @@
 ROWS = 16
 FIRST_SLOTS = 72
 FIRST_STEP = 36
-LAST_STEP = 48
+LAST_STEP = 44
 NEAR_STEP = 40
-FAR_SLOTS = 120
+FAR_SLOTS = 116
 NEAR_SLOTS = 40
 FAR_ROW = 8
 NEAR_ROW = 9

time: 44.4 us -> 44.3 us (level)
  no operation moved by 1% of the time
where the time goes in v7:
time: 44.3 us; the launch traced here: 44.2 us
  Pallas kernels  43.5 us (98%)
  local copies, waits for them, and re-layouts  0.64 us (1%)
    pallas_call x1, Pallas kernels, body(): pl.pallas_call(functools.partial(exchange_kernel, cuts, groups, cap, bloc...  22.3 us
    pallas_call x1, Pallas kernels, body(): pl.pallas_call(functools.partial(finish_kernel, cuts, groups, cap, blocks...  21.1 us

profile of v7, /device:TPU:1, one launch (start us, length us, event | category | flops | bytes accessed | tf_op | source)
XLA Modules:
  0.0 44.2 jit_solution(2398260458442487882)
XLA Ops:
  0.0 0.0 copy-start
  0.0 22.3 %exchange.1 = (f32[32,896]{1,0:T(8,128)S(1)}, f32[16,4,768]{2,1,0:T(4,128)S(1)}, s32[128,128]{1,0:T(8,128)S(1)}, s32[32,128]{1,0:T(8,128)S(1)}, s32[1,128]{1,0:T...) custom-call(f32[3,4096]{1,0:T(4,128)} %pos_in.1, ...), custom_call_target="tpu_custom_call" | custom-call | tf_op jit(solution)/shard_map/exchange/pallas_call | solution.py:696
  22.3 0.1 extra.1
  22.4 0.0 copy-done
  22.4 21.1 %finish.1 = f32[3,4096]{1,0:T(4,128)S(1)} custom-call(f32[32,384]{1,0:T(8,128)S(1)} %get-tuple-element.21.near_extra, f32[16,4,384]{2,1,0:T(4,128)S(1)} %get-tuple-element.22.far_extra, s32[32,128]{1,0:T(8,128)S(1)} %get-tuple-element.17.codes_in, s32[128,128]{1,0:T(8,128)S(1)} %get-tuple-element.23.asked, f32[32,896]{1,0:T(8,128)S(1)} %get-tuple-element.18.data, ...), custom_call_target="tpu_custom_call" | custom-call | tf_op jit(solution)/shard_map/finish/pallas_call | solution.py:752
  43.5 0.6 %copy.8 = f32[3,4096]{1,0:T(4,128)} copy(f32[3,4096]{1,0:T(4,128)S(1)} %finish.1) | data formatting | bytes 98304
Async XLA Ops:
  0.0 22.4 %copy-start = (f32[3,3]{1,0:T(4,128)S(1)}, f32[3,3]{1,0:T(4,128)}, u32[]{:S(2)}) copy-start(f32[3,3]{1,0:T(4,128)} %stress.1) | copy-start | bytes 112

commit v8 on v7

--- a/solution.py
+++ b/solution.py
@@ -13,6 +13,7 @@
 FIRST_ASK = 64
 ROWS = 16
 FIRST_SLOTS = 72
+LATER_HOPS = (8, 6, 10, 1, 15, 4, 12, 2, 14, 0)
 FIRST_STEP = 36
 LAST_STEP = 44
 NEAR_STEP = 40
@@ -202,8 +203,9 @@
 
 
 def partner(i, me, rho, groups, cuts):
-    half = groups // 2
-    hop = jnp.where(lax.rem(i, 2) == 0, half + lax.div(i, 2), half - lax.div(i + 1, 2))
+    hop = jnp.where(lax.rem(i, 2) == 0, 7 - i, 8 + i)
+    for at, other in enumerate(LATER_HOPS):
+        hop = jnp.where(i == 6 + at, other, hop)
     m = lax.rem(lax.div(me, cuts) + hop, groups)
     return m, m * cuts + rho
 
@@ -287,7 +289,7 @@
     rank = prefix(near) - cut * part_size
     mine_near = near & (rank >= 0) & (rank < part_size)
     hop = ((owner >> 2) - slot_of_me) & 15
-    distant = (hop >= 4) & (hop < 12)
+    distant = ((hop & 1) == 1) & (hop >= 3) & (hop < 14) | (hop == 8) | (hop == 6)
     mine_first = mine_far & distant
     mine_last = mine_far & jnp.logical_not(distant)
     far_spot = jnp.where(distant, prefix(mine_first), count(mine_first) + prefix(mine_last))

time: 44.3 us -> 44.3 us (level)
  no operation moved by 1% of the time
where the time goes in v8:
time: 44.3 us; the launch traced here: 44.2 us
  Pallas kernels  43.5 us (98%)
  local copies, waits for them, and re-layouts  0.64 us (1%)
    pallas_call x1, Pallas kernels, body(): pl.pallas_call(functools.partial(exchange_kernel, cuts, groups, cap, bloc...  22.5 us
    pallas_call x1, Pallas kernels, body(): pl.pallas_call(functools.partial(finish_kernel, cuts, groups, cap, blocks...  20.8 us

profile of v8, /device:TPU:1, one launch (start us, length us, event | category | flops | bytes accessed | tf_op | source)
XLA Modules:
  0.0 44.2 jit_solution(11493114374735278358)
XLA Ops:
  0.0 0.0 copy-start
  0.0 22.5 %exchange.1 = (f32[32,896]{1,0:T(8,128)S(1)}, f32[16,4,768]{2,1,0:T(4,128)S(1)}, s32[128,128]{1,0:T(8,128)S(1)}, s32[32,128]{1,0:T(8,128)S(1)}, s32[1,128]{1,0:T...) custom-call(f32[3,4096]{1,0:T(4,128)} %pos_in.1, ...), custom_call_target="tpu_custom_call" | custom-call | tf_op jit(solution)/shard_map/exchange/pallas_call | solution.py:698
  22.5 0.1 extra.1
  22.7 0.0 copy-done
  22.7 20.8 %finish.1 = f32[3,4096]{1,0:T(4,128)S(1)} custom-call(f32[32,384]{1,0:T(8,128)S(1)} %get-tuple-element.21.near_extra, f32[16,4,384]{2,1,0:T(4,128)S(1)} %get-tuple-element.22.far_extra, s32[32,128]{1,0:T(8,128)S(1)} %get-tuple-element.17.codes_in, s32[128,128]{1,0:T(8,128)S(1)} %get-tuple-element.23.asked, f32[32,896]{1,0:T(8,128)S(1)} %get-tuple-element.18.data, ...), custom_call_target="tpu_custom_call" | custom-call | tf_op jit(solution)/shard_map/finish/pallas_call | solution.py:754
  43.5 0.6 %copy.8 = f32[3,4096]{1,0:T(4,128)} copy(f32[3,4096]{1,0:T(4,128)S(1)} %finish.1) | data formatting | bytes 98304
Async XLA Ops:
  0.0 22.7 %copy-start = (f32[3,3]{1,0:T(4,128)S(1)}, f32[3,3]{1,0:T(4,128)}, u32[]{:S(2)}) copy-start(f32[3,3]{1,0:T(4,128)} %stress.1) | copy-start | bytes 112
